TPU v7x, 32 devices: a whole 2x2x4 slice. The times are simulated.
32 devices in a mesh: client: 16 (over z, y, core), mp: 2 (over x).
Axes of the slice: x: 2, y: 2, z: 4, core: 2. Of those that a mesh axis runs over, the one named last changes fastest.
Arguments:
- hidden: bfloat16 [16, 4, 128, 7168], P('client', None, None, 'mp'), may hold values from -6 to 6
- weight: bfloat16 [16, 7168, 2048], P('client', 'mp'), may hold values from -0.0625 to 0.0625
- target: bfloat16 [16, 4, 128, 2048], P('client', None, 'mp'), may hold values from -6 to 6
- router_prob: float32 [16, 4, 128], P('client', None, 'mp'), may hold values from 0.2 to 1
- routes: int32 [16, 4, 128, 2], P('client', None, 'mp'), may hold values from 0 to 7, all different within a row
- assign: int32 [16, 1], replicated, may hold values from 0 to 3
Outputs:
- merged_weight: bfloat16 [16, 7168, 2048], P('client', 'mp')
Inputs may be any that keep to these rules, and one draw needn't show every extreme that they name: `routes`: each token names two different experts; the given weights are those of expert 0. `assign`: every cluster has at least one client.
All inputs are finite; a program needn't handle non-finite values.
Results may differ from a plain program's by a relative error of at most 0.0044.
The roundings to bfloat16 on the way count: a program that leaves them out, or rounds other values in their place, can miss the bound.
Values may be sent and summed in bfloat16 or wider, within the bound.
No kernel may reach another device: no remote copies, remote signals or barrier semaphores. Data moves between devices by JAX's collectives and lax.ppermute only.
A program may use at most 256 MiB of HBM per device.

v0:
```python
import jax
import jax.numpy as jnp
from jax import lax
from jax.sharding import PartitionSpec as P

D = 2048
FFW = 7168
NB = 4
CLUSTERS = 4


EPS = 1e-06
FLOOR = 0.1


def body(hidden, weight, target, router_prob, routes, assign):
    local_weight = weight[0]
    fisher = jnp.zeros(local_weight.shape, jnp.float32)
    for batch in range(NB):
        batch_hidden = hidden[0, batch]
        outputs = lax.psum_scatter(
            jnp.dot(batch_hidden, local_weight, preferred_element_type=jnp.float32),
            "mp",
            scatter_dimension=0,
            tiled=True,
        )
        token_weight = jnp.where(
            jnp.any(routes[0, batch] == 0, axis=-1), router_prob[0, batch], 0.0
        )
        grad_out = (
            token_weight[:, None] * (outputs - target[0, batch].astype(jnp.float32))
        ).astype(jnp.bfloat16)
        grad = lax.dot_general(
            batch_hidden,
            lax.all_gather(grad_out, "mp", axis=0, tiled=True),
            (((0,), (0,)), ((), ())),
            preferred_element_type=jnp.float32,
        )
        fisher = fisher + grad * grad
    total_fisher = lax.psum(jnp.sum(fisher), "mp")
    mean_fisher = total_fisher / (FFW * D)
    a_weight = (fisher / (mean_fisher + EPS) + FLOOR).astype(jnp.bfloat16)
    got_a, got_w = (
        lax.all_to_all(a_weight[None], "client", split_axis=1, concat_axis=0, tiled=True),
        lax.all_to_all(local_weight[None], "client", split_axis=1, concat_axis=0, tiled=True),
    )
    member_table = (assign[:, 0][:, None] == jnp.arange(CLUSTERS)[None, :]).astype(jnp.float32)
    a_float = got_a.astype(jnp.float32)
    weighted = a_float * got_w.astype(jnp.float32)
    num_part = jnp.einsum("sk,srd->krd", member_table, weighted, precision=lax.Precision.HIGHEST)
    den_part = jnp.einsum("sk,srd->krd", member_table, a_float, precision=lax.Precision.HIGHEST)
    merged = (num_part / den_part).astype(jnp.bfloat16)
    own_cluster = lax.dynamic_index_in_dim(
        assign[:, 0], lax.axis_index("client"), 0, keepdims=False
    )
    every_cluster = lax.all_gather(merged, "client", axis=1, tiled=True)
    result = lax.dynamic_index_in_dim(every_cluster, own_cluster, 0, keepdims=True)
    return result


def solution(mesh):
    placed = (
        P("client", None, None, "mp"),
        P("client", "mp", None),
        P("client", None, "mp", None),
        P("client", None, "mp"),
        P("client", None, "mp", None),
        P(),
    )
    return jax.shard_map(
        body, mesh=mesh, in_specs=placed, out_specs=P("client", "mp", None), check_vma=False
    )
```

profile of v0, /device:TPU:0, one launch (start us, length us, event | category | flops | bytes accessed | tf_op | source)
XLA Modules:
  0.0 1338.6 jit_solution(13268876566863268346)
XLA Ops:
  6.5 25.8 %copy.34 = bf16[1,3584,2048]{2,0,1:T(2,128)(2,1)} copy(bf16[1,3584,2048]{2,1,0:T(8,128)(2,1)} %param.7) | data formatting | bytes 29360128 | tf_op args[1]
  32.9 87.9 %reduce.6 = bf16[3584,2048]{1,0:T(8,128)(2,1)} reduce(bf16[3584,1,2048]{2,1,0:T(2,128)(2,1)} %bitcast.76, bf16[]{:T(256)} %broadcast.39), dimensions={1}, to_apply=%bitcast.73.reduce_sub_computation | reduce | bytes 29360130
  120.8 19.2 %reshape.62 = bf16[16,2,229376]{2,1,0:T(2,128)(2,1)} reshape(bf16[3584,2048]{1,0:T(8,128)(2,1)} %reduce.6) | data formatting | bytes 29360128
  182.4 18.1 %reduce-scatter.5.cloned.1.call-done = f32[64,2048]{1,0:T(8,128)} async-done(((f32[128,2048]{1,0:T(8,128)}), f32[64,2048]{1,0:T(8,128)}) %reduce-scatter.5.cloned.1.call-update) | async-done | bytes 524304 | tf_op jit(solution)/shard_map/reduce_scatter | solution.py:21
  200.4 22.6 %reduce-scatter.7.cloned.1.call-done = f32[64,2048]{1,0:T(8,128)} async-done(((f32[128,2048]{1,0:T(8,128)}), f32[64,2048]{1,0:T(8,128)}) %reduce-scatter.7.cloned.1.call-update) | async-done | bytes 524304 | tf_op jit(solution)/shard_map/reduce_scatter | solution.py:21
  223.0 22.5 %reduce-scatter.9.cloned.1.call-done = f32[64,2048]{1,0:T(8,128)} async-done(((f32[128,2048]{1,0:T(8,128)}), f32[64,2048]{1,0:T(8,128)}) %reduce-scatter.9.cloned.1.call-update) | async-done | bytes 524304 | tf_op jit(solution)/shard_map/reduce_scatter | solution.py:21
  278.2 13.0 fusion.17
  302.8 11.7 fusion.23
  314.6 40.1 %fusion.47 = (f32[]{:T(128)}, f32[2048,3584]{1,0:T(8,128)}) fusion(bf16[128,2048]{1,0:T(8,128)(2,1)S(1)} %all_gather.18, bf16[1,4,128,3584]{3,2,1,0:T(8,128)(2,1)} %param.6, f32[2048,3584]{1,0:T(8,128)} %fusion.17, f32[2048,3584]{1,0:T(8,128)} %fusion.20, f32[2048,3584]{1,0:T(8,128)} %fusion.23), kind=kOutput, calls=%fused_computation.62 | convolution fusion | flops 1937768448 | bytes 118882304 | tf_op jit(solution)/shard_map/dot_general | solution.py:33
  361.2 17.4 %fusion.12 = bf16[1,3584,2048]{1,2,0:T(8,128)(2,1)} fusion(f32[2048,3584]{1,0:T(8,128)} %get-tuple-element.18, f32[]{:T(128)S(6)} %add.45), kind=kLoop, calls=%fused_computation.15 | loop fusion | flops 22020096 | bytes 44040196 | tf_op jit(solution)/shard_map/broadcast_in_dim | solution.py:44
  378.6 62.4 %copy.20 = bf16[1,3584,2048]{2,0,1:T(2,128)(2,1)} copy(bf16[1,3584,2048]{1,2,0:T(8,128)(2,1)} %fusion.12) | data formatting | bytes 29360128 | tf_op jit(solution)/shard_map/broadcast_in_dim | solution.py:44
  441.0 87.9 %reduce.5 = bf16[3584,2048]{1,0:T(8,128)(2,1)} reduce(bf16[3584,1,2048]{2,1,0:T(2,128)(2,1)} %bitcast.77, bf16[]{:T(256)} %broadcast.39), dimensions={1}, to_apply=%bitcast.62.reduce_sub_computation | reduce | bytes 29360130
  528.9 19.2 %reshape.60 = bf16[16,2,229376]{2,1,0:T(2,128)(2,1)} reshape(bf16[3584,2048]{1,0:T(8,128)(2,1)} %reduce.5) | data formatting | bytes 29360128
  554.1 22.8 %reshape.63 = bf16[3584,1,2048]{2,1,0:T(2,128)(2,1)} reshape(bf16[16,2,229376]{2,1,0:T(2,128)(2,1)} %all-to-all-done.1) | data formatting | bytes 29360128
  576.9 21.5 %copy.22 = bf16[1,3584,2048]{2,1,0:T(8,128)(2,1)} copy(bf16[1,3584,2048]{2,0,1:T(2,128)(2,1)} %bitcast.78) | data formatting | bytes 29360128 | tf_op jit(solution)/shard_map/all_to_all | solution.py:45
  598.4 215.7 %all-to-all-done = bf16[16,2,229376]{2,1,0:T(2,128)(2,1)} async-done(((bf16[16,2,229376]{2,1,0:T(2,128)(2,1)}), bf16[16,2,229376]{2,1,0:T(2,128)(2,1)}, u32[]{:S(2)}, u32[]{:S(2)}) %all-to-all-start) | async-done | bytes 14680096 | tf_op jit(solution)/shard_map/all_to_all | solution.py:44
  814.1 22.8 %reshape.61 = bf16[3584,1,2048]{2,1,0:T(2,128)(2,1)} reshape(bf16[16,2,229376]{2,1,0:T(2,128)(2,1)} %all-to-all-done) | data formatting | bytes 29360128
  836.9 19.5 %copy.26 = bf16[1,3584,2048]{2,1,0:T(8,128)(2,1)S(1)} copy(bf16[1,3584,2048]{2,0,1:T(2,128)(2,1)} %bitcast.79) | data formatting | bytes 29360128
  856.5 14.9 %convert_multiply_fusion = f32[16,224,2048]{2,1,0:T(8,128)} fusion(bf16[16,224,2048]{2,1,0:T(8,128)(2,1)S(1)} %bitcast.80, bf16[16,224,2048]{2,1,0:T(8,128)(2,1)S(1)} %bitcast.74), kind=kLoop, calls=%fused_computation | loop fusion | flops 22020096 | bytes 58720256 | tf_op jit(solution)/shard_map/mul | solution.py:49
  871.4 24.6 %fusion.10 = f32[4,224,2048]{2,0,1:T(4,128)} fusion(bf16[16,224,2048]{2,1,0:T(8,128)(2,1)} %bitcast.75, s32[16]{0:T(128)S(1)} %bitcast.81), kind=kOutput, calls=%fused_computation.13 | convolution fusion | flops 58720320 | bytes 22020160 | tf_op jit(solution)/shard_map/sk,srd->krd/dot_general | solution.py:51
  896.1 37.0 %divide_convert_fusion = bf16[4,224,2048]{2,0,1:T(4,128)(2,1)} fusion(f32[4,224,2048]{2,0,1:T(4,128)} %fusion.10, f32[16,224,2048]{2,1,0:T(8,128)} %convert_multiply_fusion, s32[16]{0:T(128)S(1)} %bitcast.82), kind=kOutput, calls=%fused_computation.16 | convolution fusion | flops 355991616 | bytes 40370240 | tf_op jit(solution)/shard_map/sk,srd->krd/dot_general | solution.py:50
  935.7 340.2 %all-gather.2.cloned.1.call-done = bf16[4,3584,2048]{2,0,1:T(4,128)(2,1)} async-done(((bf16[4,224,2048]{2,0,1:T(4,128)(2,1)}), bf16[4,3584,2048]{2,0,1:T(4,128)(2,1)}) %all-gather.2.cloned.1.call-update) | async-done | bytes 58720272 | tf_op jit(solution)/shard_map/all_gather | solution.py:56
  1276.0 34.4 %constant_dynamic-slice_fusion = bf16[1,3584,2048]{2,0,1:T(2,128)(2,1)} fusion(bf16[4,3584,2048]{2,0,1:T(4,128)(2,1)} %all-gather.2.cloned.1.call-done, s32[]{:T(128)S(6)} %select_n.42), kind=kLoop, calls=%fused_computation.60 | loop fusion | bytes 29360132 | tf_op jit(solution)/shard_map/jit(dynamic_index_in_dim)/dynamic_slice | solution.py:57
  1310.4 21.5 %copy.25 = bf16[1,3584,2048]{2,1,0:T(8,128)(2,1)} copy(bf16[1,3584,2048]{2,0,1:T(2,128)(2,1)} %constant_dynamic-slice_fusion) | data formatting | bytes 29360128 | tf_op jit(solution)/shard_map/jit(dynamic_index_in_dim)/dynamic_slice | solution.py:57
  (43 shorter events, 99.7 us)
Async XLA Ops:
  140.0 408.1 %all-to-all-start.1 = ((bf16[16,2,229376]{2,1,0:T(2,128)(2,1)}), bf16[16,2,229376]{2,1,0:T(2,128)(2,1)}, u32[]{:S(2)}, u32[]{:S(2)}) async-start(bf16[16,2,229376]{2,1,0:T(2,128)(2,1)} %reshape.62), calls=%async_computation.5 | async-start | bytes 29360128 | tf_op jit(solution)/shard_map/all_to_all | solution.py:45
  147.4 34.9 %reduce-scatter.11.cloned.1.call-start = ((), (), s32[]{:S(2)}) async-start(), calls=%async_computation.9 | async-start | bytes 1572864 | tf_op jit(solution)/shard_map/reduce_scatter | solution.py:21
  156.0 44.4 %reduce-scatter.5.cloned.1.call-start = ((), (), s32[]{:S(2)}) async-start(), calls=%async_computation.6 | async-start | bytes 1572864 | tf_op jit(solution)/shard_map/reduce_scatter | solution.py:21
  164.6 58.4 %reduce-scatter.7.cloned.1.call-start = ((), (), s32[]{:S(2)}) async-start(), calls=%async_computation.7 | async-start | bytes 1572864 | tf_op jit(solution)/shard_map/reduce_scatter | solution.py:21
  173.5 8.8 copy-start.4
  173.5 8.8 copy-start.5
  173.5 72.1 %copy-start.3 = (bf16[1,4,64,2048]{3,2,1,0:T(8,128)(2,1)S(1)}, bf16[1,4,64,2048]{3,2,1,0:T(8,128)(2,1)}, u32[]{:S(2)}) copy-start(bf16[1,4,64,2048]{3,2,1,0:T(8,128)(2,1)} %param.8) | copy-start | bytes 3145732
  173.5 72.0 %reduce-scatter.9.cloned.1.call-start = ((), (), s32[]{:S(2)}) async-start(), calls=%async_computation.8 | async-start | bytes 1572864 | tf_op jit(solution)/shard_map/reduce_scatter | solution.py:21
  278.2 13.0 copy-start.2
  548.1 266.0 %all-to-all-start = ((bf16[16,2,229376]{2,1,0:T(2,128)(2,1)}), bf16[16,2,229376]{2,1,0:T(2,128)(2,1)}, u32[]{:S(2)}, u32[]{:S(2)}) async-start(bf16[16,2,229376]{2,1,0:T(2,128)(2,1)} %reshape.60), calls=%async_computation.4 | async-start | bytes 29360128 | tf_op jit(solution)/shard_map/all_to_all | solution.py:44
  553.9 722.1 %all-gather.2.cloned.1.call-start = ((), (), s32[]{:S(2)}) async-start(), calls=%async_computation.10 | async-start | bytes 62390272 | tf_op jit(solution)/shard_map/all_gather | solution.py:56
  836.9 19.6 %copy-start.1 = (bf16[1,3584,2048]{2,1,0:T(8,128)(2,1)S(1)}, bf16[1,3584,2048]{2,1,0:T(8,128)(2,1)}, u32[]{:S(2)}) copy-start(bf16[1,3584,2048]{2,1,0:T(8,128)(2,1)} %copy.22) | copy-start | bytes 44040196
  856.5 14.9 %copy-start = (bf16[1,3584,2048]{2,1,0:T(8,128)(2,1)}, bf16[1,3584,2048]{2,1,0:T(8,128)(2,1)S(1)}, u32[]{:S(2)}) copy-start(bf16[1,3584,2048]{2,1,0:T(8,128)(2,1)S(1)} %copy.26) | copy-start | bytes 44040196
  856.5 14.9 %copy-start.6 = (s32[16,1]{0,1:T(1,128)S(1)}, s32[16,1]{0,1:T(1,128)}, u32[]{:S(2)}) copy-start(s32[16,1]{0,1:T(1,128)} %param.11) | copy-start | bytes 196
Sparse Core Ops, SparseCore 0:
  156.1 21.5 reduce-scatter.10
  180.1 20.3 reduce-scatter.4
  202.7 20.3 reduce-scatter.6
  225.2 20.3 reduce-scatter.8
  933.2 342.7 all-gather.1
where the time goes:
time: 1350 us; the launch traced here: 1340 us
  waiting for transfers between devices  619 us (46%)
  local copies, waits for them, and re-layouts  270 us (20%)
  other arithmetic  210 us (16%)
  matrix products  172 us (13%)
  blocking collectives  36.8 us (3%)
  between operations  16.1 us (1%)
  starting transfers between devices  13.7 us (1%)
    all_gather x1, waiting for transfers between devices, body(): every_cluster = lax.all_gather(merged, 'client', axis=1, tiled=True)  340 us
    all_to_all x1, waiting for transfers between devices, body(): lax.all_to_all(a_weight[None], 'client', split_axis=1, concat_axis=0, til...  216 us
    unnamed x2, other arithmetic  176 us
    unnamed x21, local copies, waits for them, and re-layouts  130 us
    dot_general x4, matrix products, body(): lax.dot_general(batch_hidden, lax.all_gather(grad_out, 'mp', axis=0, tile...  76.5 us
    reduce_scatter x4, waiting for transfers between devices, body(): lax.psum_scatter(jnp.dot(batch_hidden, local_weight, preferred_element_ty...  63.2 us
    broadcast_in_dim x1, local copies, waits for them, and re-layouts, body(): a_weight[None]  62.4 us
    dynamic_slice x2, local copies, waits for them, and re-layouts, body(): lax.dynamic_index_in_dim(every_cluster, own_cluster, 0, keepdims=True)  55.9 us
  transfers between devices with their start and end apart: 7, of which 5 were waited for; matrix products, arithmetic and copies ran while one was open for 26% of the time, Pallas kernels for 0%

commit v1 on v0

v1 whole, which is shorter than its diff:
```python
import functools

import jax
import jax.numpy as jnp
from jax import lax
from jax.experimental import pallas as pl
from jax.experimental.pallas import tpu as pltpu
from jax.sharding import PartitionSpec as P

CLUSTERS = 4
EPS = 1e-06
FLOOR = 0.1
LAYERS = 4
LEAD = 5
VMEM = 48 * 1024 * 1024
F32 = jnp.float32
BF16 = jnp.bfloat16
HUB, UPPER, COLUMN, SIDE, FIRST = range(5)


def call(kernel, grid, ids, scales, in_specs, operands, out_specs, out_shape, name, cost, **kw):
    prefetch = [ids] if scales is None else [ids, scales]
    aliases = {len(prefetch) + i: o for i, o in kw.pop("aliases", {}).items()}
    return pl.pallas_call(
        kernel,
        out_shape=out_shape,
        grid_spec=pltpu.PrefetchScalarGridSpec(
            num_scalar_prefetch=len(prefetch),
            grid=grid,
            in_specs=in_specs,
            out_specs=out_specs,
            scratch_shapes=kw.pop("scratch", []),
        ),
        input_output_aliases=aliases,
        compiler_params=pltpu.CompilerParams(vmem_limit_bytes=VMEM),
        cost_estimate=pl.CostEstimate(flops=cost[0], bytes_accessed=cost[1], transcendentals=0),
        name=name,
    )(*prefetch, *operands)


def merge_kernel(peers, parts, final, extra, ids_ref, scale_ref, *refs):
    weights, hiddens, refs = refs[: 2 * peers], refs[2 * peers : 4 * peers], refs[4 * peers :]
    grads, refs = refs[: 2 * peers * parts], refs[2 * peers * parts :]
    got_ref = refs[0] if final else None
    out_ref, num, den = refs[-3:]

    @pl.when(ids_ref[HUB] == 1)
    def _():
        if final:
            num[...] = got_ref[:CLUSTERS].astype(F32)
            den[...] = got_ref[CLUSTERS:].astype(F32)
        else:
            num[...] = jnp.zeros_like(num)
            den[...] = jnp.zeros_like(den)
        tokens = hiddens[0].shape[1] // 4
        for slot in range(2 * peers):
            fisher = None
            for batch in range(4):
                part, start = divmod(batch * tokens, grads[0].shape[0])
                grad = jnp.dot(
                    hiddens[slot][:, batch * tokens : (batch + 1) * tokens],
                    grads[slot * parts + part][start : start + tokens, :],
                    preferred_element_type=F32,
                )
                fisher = grad * grad if fisher is None else fisher + grad * grad
            a_weight = (fisher * scale_ref[slot] + FLOOR).astype(BF16).astype(F32)
            cluster = ids_ref[FIRST + slot]
            num[cluster] += a_weight * weights[slot][...].astype(F32)
            den[cluster] += a_weight
        if final:
            out_ref[...] = (num[...] / den[...]).astype(BF16)
        else:
            out_ref[:CLUSTERS] = num[...].astype(BF16)
            out_ref[CLUSTERS:] = den[...].astype(BF16)


def merge_step(ids, scales, chunk, grads, rows, half, got, planes, held, after):
    final = got is not None
    peers = len(grads) // 2
    parts = len(grads[0])
    tokens = sum(array.shape[1] for array, _ in grads[0])
    width = 256 if half % 256 == 0 else half
    tiles = half // width
    in_specs, operands = [], []
    for (array, index), row, offset in chunk["weights"]:
        operands.append(array)
        in_specs.append(
            pl.BlockSpec(
                (None, rows, width),
                lambda g, ids, sc, i=index, row=row, first=offset // width: (
                    i,
                    row,
                    first + ids[SIDE] * tiles + g,
                ),
            )
        )
    for (array, index), row in chunk["hiddens"]:
        operands.append(array)
        in_specs.append(
            pl.BlockSpec((None, rows, tokens), lambda g, ids, sc, i=index, row=row: (i, row, 0))
        )
    for slot in grads:
        for array, index in slot:
            operands.append(array)
            in_specs.append(
                pl.BlockSpec(
                    (None, array.shape[1], width),
                    lambda g, ids, sc, index=index: (index, 0, ids[SIDE] * tiles + g),
                )
            )
    if final:
        operands.append(got)
        in_specs.append(pl.BlockSpec((2 * CLUSTERS, rows, width), lambda g, ids, sc: (0, 0, g)))
    aliases = {}
    if held is not None:
        aliases = {len(operands): 0}
        operands.append(held)
        in_specs.append(pl.BlockSpec(memory_space=pl.ANY))
    for array in after:
        operands.append(array)
        in_specs.append(pl.BlockSpec(memory_space=pl.ANY))
    if final:
        place = planes // CLUSTERS - 1
        out_spec = pl.BlockSpec((CLUSTERS, rows, width), lambda g, ids, sc: (place, 0, g))
    else:
        out_spec = pl.BlockSpec((2 * CLUSTERS, rows, width), lambda g, ids, sc: (0, 0, g))
    return call(
        functools.partial(merge_kernel, peers, parts, final, len(after)),
        (tiles,),
        ids,
        scales,
        in_specs,
        operands,
        out_spec,
        jax.ShapeDtypeStruct((planes, rows, half), BF16),
        "merge_final" if final else "merge_partial",
        (4 * peers * rows * tokens * half, 4 * peers * (rows * half + rows * tokens + tokens * half)),
        aliases=aliases,
        scratch=[pltpu.VMEM((CLUSTERS, rows, width), F32)] * 2,
    )


def planes_spec(array, rows, half):
    last = array.shape[0] // CLUSTERS - 1
    return pl.BlockSpec((CLUSTERS, rows, half), lambda *_: (last, 0, 0))


def pack_kernel(up, ids_ref, mine_ref, other_ref, *refs):
    out_ref = refs[-1]
    half = mine_ref.shape[2]
    base = out_ref.shape[2] - 2 * half

    @pl.when((ids_ref[HUB] == 1) & (ids_ref[UPPER] == 0))
    def _():
        out_ref[:CLUSTERS, :, base : base + half] = other_ref[...]
        out_ref[:CLUSTERS, :, base + half :] = mine_ref[...]

    @pl.when((ids_ref[HUB] == 1) & (ids_ref[UPPER] == 1))
    def _():
        out_ref[:CLUSTERS, :, base : base + half] = mine_ref[...]
        out_ref[:CLUSTERS, :, base + half :] = other_ref[...]

    if up:

        @pl.when(ids_ref[HUB] == 0)
        def _():
            for peer, ref in enumerate(refs[:-1]):
                out_ref[peer] = ref[...]


def pack_step(ids, mine, other, source, row, rows, half, peers):
    in_specs = [planes_spec(mine, rows, half), planes_spec(other, rows, half)]
    operands = [mine, other]
    width = 2 * half
    for array, index in source:
        width = array.shape[2]
        in_specs.append(pl.BlockSpec((None, rows, width), lambda g, ids, i=index: (i, row, 0)))
        operands.append(array)
    shape = (max(peers, CLUSTERS), rows, width)
    return call(
        functools.partial(pack_kernel, bool(source)),
        (1,),
        ids,
        None,
        in_specs,
        operands,
        pl.BlockSpec(shape, lambda g, ids: (0, 0, 0)),
        jax.ShapeDtypeStruct(shape, BF16),
        "pack",
        (0, 4 * shape[0] * rows * width),
    )


def pick_kernel(peers, chunks, ids_ref, *refs):
    outs = refs[-2:]
    for index in range(chunks):
        mine_ref, other_ref, leaf_ref = refs[3 * index : 3 * index + 3]
        half = mine_ref.shape[2]
        base = leaf_ref.shape[2] - 2 * half
        for peer in range(peers):
            cluster = ids_ref[FIRST + peer]
            out_ref = outs[peer // (peers // 2)]
            to = peer % (peers // 2)

            @pl.when((ids_ref[HUB] == 1) & (ids_ref[UPPER] == 0))
            def _():
                out_ref[to, index, :, :half] = other_ref[cluster]
                out_ref[to, index, :, half:] = mine_ref[cluster]

            @pl.when((ids_ref[HUB] == 1) & (ids_ref[UPPER] == 1))
            def _():
                out_ref[to, index, :, :half] = mine_ref[cluster]
                out_ref[to, index, :, half:] = other_ref[cluster]

            @pl.when(ids_ref[HUB] == 0)
            def _():
                out_ref[to, index] = leaf_ref[cluster, :, base:]


def pick_step(ids, group, rows, half, peers):
    in_specs, operands = [], []
    for mine, other, leaf in group:
        operands += [mine, other, leaf]
        in_specs += [planes_spec(mine, rows, half), planes_spec(other, rows, half)]
        in_specs.append(pl.BlockSpec(leaf.shape, lambda *_: (0, 0, 0)))
    shape = (peers // 2, len(group), rows, 2 * half)
    return call(
        functools.partial(pick_kernel, peers, len(group)),
        (1,),
        ids,
        None,
        in_specs,
        operands,
        [pl.BlockSpec(shape, lambda g, ids: (0, 0, 0, 0))] * 2,
        [jax.ShapeDtypeStruct(shape, BF16)] * 2,
        "pick",
        (0, 16 * rows * half * len(group) * peers),
    )


def place_kernel(peers, ids_ref, *refs):
    out_ref, token_ref = refs[-2:]
    token_ref[...] = jnp.zeros_like(token_ref)
    for peer in range(peers):

        @pl.when(pl.program_id(1) == peer)
        def _(peer=peer):
            out_ref[...] = refs[peer][...]


def place_step(ids, blocks, result):
    peers = len(blocks)
    _, chunks, rows, width = blocks[0][0].shape
    step = 1 + peers
    in_specs = [
        pl.BlockSpec((None, None, rows, width), lambda c, p, ids, i=index: (i, c, 0, 0))
        for _, index in blocks
    ]
    return call(
        functools.partial(place_kernel, peers),
        (chunks, peers),
        ids,
        None,
        in_specs + [pl.BlockSpec(memory_space=pl.ANY)],
        [array for array, _ in blocks] + [result],
        [
            pl.BlockSpec((rows, width), lambda c, p, ids: (ids[c * step + 1 + p], ids[c * step])),
            pl.BlockSpec((8, 128), lambda c, p, ids: (0, 0)),
        ],
        [jax.ShapeDtypeStruct(result.shape, BF16), jax.ShapeDtypeStruct((8, 128), F32)],
        "place",
        (0, 4 * chunks * peers * rows * width),
        aliases={peers: 0},
    )


def forward_kernel(own, batches, ids_ref, hidden_ref, weight_ref, target_ref, *outs):
    total = jnp.dot(hidden_ref[...], weight_ref[...], preferred_element_type=F32)
    tokens = hidden_ref.shape[0] // batches
    span = target_ref.shape[1]
    half = batches // 2
    for part in range(2):
        out_ref = outs[part]
        out_ref[...] = total[part * half * tokens : (part + 1) * half * tokens]
        for batch in range(half):
            rows = pl.ds(pl.multiple_of(batch * tokens + ids_ref[0] * span, 8), span)
            out_ref[rows, :] = out_ref[rows, :] - target_ref[part * half + batch].astype(F32)
    if own:

        @pl.when(pl.program_id(0) == 0)
        def _():
            for batch in range(batches):
                rows = hidden_ref[batch * tokens : (batch + 1) * tokens, :]
                outs[2][batch] = lax.dot_general(
                    rows, rows, (((1,), (1,)), ((), ())), preferred_element_type=F32
                )


def forward_step(ids, flat, weight, target, block, shards, own):
    every, depth = flat.shape
    batches = target.shape[0]
    tokens = every // batches
    width = min(block, 256)
    tiles = block // width
    count = tiles if own else tiles * (shards - 1)
    columns = lambda g, ids: ids[1 + g // tiles] * tiles + g % tiles
    out_specs = [pl.BlockSpec((every // 2, width), lambda g, ids: (0, g))] * 2
    out_shape = [jax.ShapeDtypeStruct((every // 2, count * width), F32)] * 2
    if own:
        out_specs.append(pl.BlockSpec((batches, tokens, tokens), lambda g, ids: (0, 0, 0)))
        out_shape.append(jax.ShapeDtypeStruct((batches, tokens, tokens), F32))
    return call(
        functools.partial(forward_kernel, own, batches),
        (count,),
        ids.astype(jnp.int32),
        None,
        [
            pl.BlockSpec((every, depth), lambda g, ids: (0, 0)),
            pl.BlockSpec((depth, width), lambda g, ids: (0, columns(g, ids))),
            pl.BlockSpec((batches, target.shape[1], width), lambda g, ids: (0, 0, columns(g, ids))),
        ],
        [flat, weight, target],
        out_specs,
        out_shape,
        "forward",
        (2 * every * depth * count * width, 2 * depth * (every + count * width)),
    )


def cut_kernel(count, every, ids_ref, weight_ref, *refs):
    outs = refs[-2:]
    for index in range(2):

        @pl.when(pl.program_id(0) // count == index)
        def _(index=index):
            if every:
                outs[index][:, :every] = refs[0][...]
            outs[index][:, every:] = weight_ref[...]


def cut_step(ids, weight, turned, size, chunks, block, peers, after):
    count = peers // 2
    in_specs = [pl.BlockSpec((size, block), lambda p, c, ids: (ids[1 + p] + c, ids[0]))]
    operands = [weight]
    every = 0
    if turned is not None:
        every = turned.shape[1]
        in_specs.append(pl.BlockSpec((size, every), lambda p, c, ids: (ids[1 + p] + c, 0)))
        operands.append(turned)
    for array in after:
        operands.append(array)
        in_specs.append(pl.BlockSpec(memory_space=pl.ANY))
    shape = (count, chunks * size, every + block)
    spec = lambda index: pl.BlockSpec((None, size, every + block), index)
    return call(
        functools.partial(cut_kernel, count, every),
        (peers, chunks),
        ids,
        None,
        in_specs,
        operands,
        [
            spec(lambda p, c, ids: (jnp.minimum(p, count - 1), jnp.where(p < count, c, chunks - 1), 0)),
            spec(lambda p, c, ids: (jnp.maximum(p - count, 0), jnp.where(p < count, 0, c), 0)),
        ],
        [jax.ShapeDtypeStruct(shape, BF16)] * 2,
        "cut",
        (0, 8 * count * shape[1] * shape[2]),
    )


def body(clients, shards, hidden, weight, target, router_prob, routes, assign):
    batches, tokens, depth = hidden.shape[1:]
    width = weight.shape[2]
    peers = clients // LAYERS
    rows = depth // peers
    block = width // shards
    half = block // 2
    pieces = max(1, 14 // shards)
    if rows % (16 * pieces):
        pieces = 1
    size = rows // pieces
    every = batches * tokens
    chunks = [(j, r) for j in range(shards) for r in range(pieces)]
    count = len(chunks)
    lead = min(LEAD, count)

    client = lax.axis_index("client")
    shard = lax.axis_index("mp")
    layer, place = client // peers, client % peers
    is_hub = (layer == 1) | (layer == 2)
    upper = (layer >= 2).astype(jnp.int32)
    ranks = place ^ jnp.arange(peers)

    def swap(k):
        return [(z * peers + q, z * peers + (q ^ k)) for z in range(LAYERS) for q in range(peers)]

    def between(links):
        return [(a * peers + q, b * peers + q) for a, b in links for q in range(peers)]

    to_peer = lambda array, k: lax.ppermute(array, "client", swap(k))
    leaf_to_hub = lambda array: lax.ppermute(array, "client", between([(0, 1), (3, 2)]))
    leaf_and_hub = lambda array: lax.ppermute(
        array, "client", between([(0, 1), (1, 0), (2, 3), (3, 2)])
    )
    hub_to_hub = lambda array: lax.ppermute(array, "client", between([(1, 2), (2, 1)]))
    ahead = lambda j: [(s, (s + j) % shards) for s in range(shards)]
    behind = lambda j: [(s, (s - j) % shards) for s in range(shards)]

    def exchange(held):
        held = list(held)
        bit = peers // 2
        while bit:
            moved = [k for k in range(peers) if k & bit]
            arrays = {id(held[k][0]) for k in moved}
            if len(arrays) == 1 and held[moved[0]][0].shape[0] == len(moved):
                array = held[moved[0]][0]
            else:
                array = jnp.stack([held[k][0][held[k][1]] for k in moved])
            got = to_peer(array, bit)
            for i, k in enumerate(moved):
                held[k] = (got, i)
            bit //= 2
        return held

    def gather_peers(arrays):
        held = [{0: (array[None], 0)} for array in arrays]
        bit = peers // 2
        while bit:
            keys = [(n, k) for n in range(len(held)) for k in held[n]]
            if bit == peers // 2:
                for n, k in keys:
                    array, i = held[n][k]
                    held[n][k ^ bit] = (to_peer(array[i][None], bit), 0)
            else:
                got = to_peer(jnp.stack([held[n][k][0][held[n][k][1]] for n, k in keys]), bit)
                for i, (n, k) in enumerate(keys):
                    held[n][k ^ bit] = (got, i)
            bit //= 2
        return [[h[k] for k in range(peers)] for h in held]

    local_weight = weight[0]
    flat = hidden[0].reshape(every, depth)
    turned = flat.T
    others_at = jnp.concatenate([shard[None], (shard + jnp.arange(1, shards)) % shards])
    others = forward_step(others_at, flat, local_weight, target[0], block, shards, False)
    mine_at = jnp.stack([shard, shard])
    *mine, hidden_gram = forward_step(mine_at, flat, local_weight, target[0], block, shards, True)
    hidden_gram = lax.psum(hidden_gram, "mp")
    token_weight = jnp.where(jnp.any(routes[0] == 0, axis=-1), router_prob[0], 0.0)
    token_weight = jnp.stack(
        [token_weight] + [lax.ppermute(token_weight, "mp", behind(j)) for j in range(1, shards)]
    )
    token_weight = token_weight[(jnp.arange(shards) - shard) % shards]
    token_weight = token_weight.transpose(1, 0, 2).reshape(every, 1)
    grad_parts = []
    for part in range(2):
        total = mine[part]
        for j in range(1, shards):
            total = total + lax.ppermute(
                others[part][:, (j - 1) * block : j * block], "mp", ahead(j)
            )
        grad = token_weight[part * every // 2 : (part + 1) * every // 2] * total
        grad_parts.append(grad.astype(BF16))

    def spread_grads(parts):
        many = [gather_peers([part, leaf_to_hub(part)]) for part in parts]
        return [[many[p][side][k] for p in range(len(parts))] for side in range(2) for k in range(peers)]

    grads = {0: spread_grads(grad_parts)}

    gram = sum(
        jnp.sum(
            hidden_gram[part * batches // 2 : (part + 1) * batches // 2]
            * jnp.einsum(
                "btd,bsd->bts", *[g.reshape(batches // 2, tokens, block)] * 2, preferred_element_type=F32
            )
        )
        for part, g in enumerate(grad_parts)
    )
    gram = jnp.full((8, 128), gram)
    total = gram
    for j in range(1, shards):
        total = total + lax.ppermute(gram, "mp", ahead(j))
    totals = [a[i, 0, 0] for side in gather_peers([total, leaf_to_hub(total)]) for a, i in side]
    scales = 1.0 / (jnp.stack(totals) / (depth * shards * width) + EPS)

    cluster_of = assign[:, 0].astype(jnp.int32)
    slot_clients = jnp.concatenate(
        [layer * peers + ranks, jnp.where(upper == 1, 3, 0) * peers + ranks]
    )
    slot_clusters = cluster_of[slot_clients]

    own, far = {}, {}

    def spread(j, low, high, after):
        order = [place ^ (k + peers // 2) % peers for k in range(peers)]
        at = jnp.stack([(shard + j) % shards] + [q * pieces + low for q in order]).astype(jnp.int32)
        hi, lo = cut_step(
            at, local_weight, None if j else turned, size, high - low, block, peers, after
        )
        parts = peers // 2
        held = exchange([((lo, hi)[k // parts], k % parts) for k in range(peers)])
        numbers = [j * pieces + r for r in range(low, high)]
        for i, c in enumerate(numbers):
            own[c] = (held, i)
        early = sum(c < lead for c in numbers)
        if early:
            array = leaf_to_hub(jnp.stack([a[i, : early * size] for a, i in held]))
            for i in range(early):
                far[numbers[i]] = ([(array, k) for k in range(peers)], i)
        return held[-1][0]

    if pieces > 3:
        spread(0, 0, 1, [])
        spread(0, 1, 3, [others[0]])
        last = spread(0, 3, pieces, [grads[0][peers // 2][1][0]])
    else:
        last = spread(0, 0, pieces, [])
        for j in range(1, shards):
            last = spread(j, 0, pieces, [last])

    def ids_for(c, side):
        head = [is_hub, upper, (shard + chunks[c][0]) % shards, side]
        return jnp.concatenate([jnp.stack([v.astype(jnp.int32) for v in head]), slot_clusters])

    def merge(c, side, got, planes, held, after=()):
        j, r = chunks[c]
        weights, hiddens = [], []
        for table in (own, far):
            slots, row = table[c]
            weights += [(slot, row, 0 if j else every) for slot in slots]
            slots, row = table[r]
            hiddens += [(slot, row) for slot in slots]
        chunk = dict(weights=weights, hiddens=hiddens)
        return merge_step(
            ids_for(c, side), scales, chunk, grads[j], size, half, got, planes, held, after
        )

    result = jnp.zeros((depth, width), BF16)
    sent, got, leaf, tokens_of = {}, {}, {}, {}
    waiting = []

    def finish(c):
        nonlocal result, waiting
        later = c + lead
        source, row = own[later] if later < count else ([], 0)
        packed = pack_step(
            ids_for(c, upper), sent[c + 2], got[c + 2], source, row, size, half, peers
        )
        leaf[c] = leaf_and_hub(packed)
        if later < count:
            far[later] = ([(leaf[c], k) for k in range(peers)], 0)
        waiting.append(c)
        if len(waiting) == 2 or c >= count - 2:
            lo, hi = pick_step(
                ids_for(c, upper),
                [(sent[w + 2], got[w + 2], leaf[w]) for w in waiting],
                size,
                half,
                peers,
            )
            parts = peers // 2
            held = exchange([((lo, hi)[k // parts], k % parts) for k in range(peers)])
            where = []
            for w in waiting:
                where.append(((shard + chunks[w][0]) % shards)[None])
                where.append(ranks * pieces + chunks[w][1])
            result, token = place_step(jnp.concatenate(where).astype(jnp.int32), held, result)
            for w in waiting:
                tokens_of[w] = token
            waiting = []

    for t in range(count + 2):
        if t >= 3:
            finish(t - 3)
        planes = (2 if t < count else 0) * CLUSTERS + (CLUSTERS if t >= 2 else 0)
        buffer = None
        if t >= 2:
            buffer = merge(t - 2, 1 - upper, got[t - 2], planes, None)
        if t < count:
            after = []
            if t - 6 in leaf:
                after.append(leaf[t - 6])
            if t - 8 in tokens_of:
                after.append(tokens_of[t - 8])
            buffer = merge(t, upper, None, planes, buffer, after)
        sent[t] = buffer
        got[t] = hub_to_hub(buffer)
        j = 1 + t * (shards - 1) // max(1, pieces * (shards - 1))
        if t % pieces == 0 and j < shards and pieces > 3:
            last = spread(j, 0, pieces, [last, got[t]])
        if t % pieces == min(2, pieces - 1) and j < shards:
            grads[j] = spread_grads([lax.ppermute(g, "mp", behind(j)) for g in grad_parts])
    finish(count - 1)
    return result[None]


def solution(mesh):
    placed = (
        P("client", None, None, "mp"),
        P("client", "mp", None),
        P("client", None, "mp", None),
        P("client", None, "mp"),
        P("client", None, "mp", None),
        P(),
    )
    return jax.shard_map(
        functools.partial(body, mesh.shape["client"], mesh.shape["mp"]),
        mesh=mesh,
        in_specs=placed,
        out_specs=P("client", "mp", None),
        check_vma=False,
    )
```

time: 1350 us -> 969 us (0.72)
  waiting for transfers between devices: 619 us -> 305 us
  Pallas kernels: 0 us -> 259 us
  starting transfers between devices: 13.7 us -> 258 us
  local copies, waits for them, and re-layouts: 270 us -> 80.6 us
  other arithmetic: 210 us -> 29.4 us
  matrix products: 172 us -> 2.91 us
  blocking collectives: 36.8 us -> 0 us
    all_gather x1 -> x0, waiting for transfers between devices: 340 us -> none  [body(): every_cluster = lax.all_gather(merged, 'client', axis=1, tiled=True)]
    ppermute x0 -> x83, waiting for transfers between devices: none -> 305 us  [the longest x39 181 us: body(): to_peer = lambda array, k: lax.ppermute(array, 'client', swap(k))]
    pallas_call x0 -> x64, Pallas kernels: none -> 259 us  [call(): pl.pallas_call(kernel, out_shape=out_shape, grid_spec=pltpu.PrefetchScala...]
    ppermute x0 -> x83, starting transfers between devices: none -> 258 us  [the longest x14 160 us: body(): lax.ppermute(array, 'client', between([(0, 1), (1, 0), (2, 3), (3, 2)]))]
    all_to_all x2 -> x0, waiting for transfers between devices: 216 us -> none  [the longest x1 216 us: body(): lax.all_to_all(a_weight[None], 'client', split_axis=1, concat_axis=0, til...]
    unnamed x2 -> x0, other arithmetic: 176 us -> none
    dot_general x10 -> x2, matrix products: 172 us -> 2.91 us  [body(): jnp.einsum('btd,bsd->bts', *[g.reshape(batches // 2, tokens, block)] * 2,...]
    unnamed x21 -> x276, local copies, waits for them, and re-layouts: 130 us -> 41.9 us
  transfers between devices with their start and end apart: 7 -> 84, of which waited for: 5 -> 26; matrix products, arithmetic and copies ran while one was open for 26% -> 7% of each run, Pallas kernels for 0% -> 27%
where the time goes in v1:
time: 969 us; the launch traced here: 953 us
  waiting for transfers between devices  305 us (31%)
  Pallas kernels  259 us (27%)
  starting transfers between devices  258 us (27%)
  local copies, waits for them, and re-layouts  80.6 us (8%)
  other arithmetic  29.4 us (3%)
  between operations  16.8 us (2%)
    pallas_call x64, Pallas kernels, call(): pl.pallas_call(kernel, out_shape=out_shape, grid_spec=pltpu.PrefetchScala...  259 us
    ppermute x39, waiting for transfers between devices, body(): to_peer = lambda array, k: lax.ppermute(array, 'client', swap(k))  181 us
    ppermute x14, starting transfers between devices, body(): lax.ppermute(array, 'client', between([(0, 1), (1, 0), (2, 3), (3, 2)]))  160 us
    ppermute x8, waiting for transfers between devices, body(): lax.ppermute(array, 'client', between([(0, 1), (3, 2)]))  98 us
    ppermute x8, starting transfers between devices, body(): lax.ppermute(array, 'client', between([(0, 1), (3, 2)]))  47.6 us
    unnamed x276, local copies, waits for them, and re-layouts  41.9 us
    ppermute x16, starting transfers between devices, body(): lax.ppermute(array, 'client', between([(1, 2), (2, 1)]))  23 us
    ppermute x14, waiting for transfers between devices, body(): lax.ppermute(array, 'client', between([(0, 1), (1, 0), (2, 3), (3, 2)]))  20.3 us
  transfers between devices with their start and end apart: 84, of which 26 were waited for; matrix products, arithmetic and copies ran while one was open for 7% of the time, Pallas kernels for 27%

profile of v1, /device:TPU:0, one launch (start us, length us, event | category | flops | bytes accessed | tf_op | source)
XLA Modules:
  0.0 952.7 jit_solution(7074062305769095754)
XLA Ops:
  34.9 10.2 %forward.2 = (f32[256,1024]{1,0:T(8,128)S(1)}, f32[256,1024]{1,0:T(8,128)S(1)}, f32[4,128,128]{2,1,0:T(8,128)}) custom-call(s32[2]{0:T(128)S(1)} %get-tuple-element.117.ids_ref, bf16[512,3584]{1,0:T(8,128)(2,1)} %bitcast.207, bf16[3584,2048]{1,0:T(8,128)(2,1)} %bitcast.201, bf16[4,64,2048]{2,1,0:T(8,128)(2,1)S(1)} %bitcast.198), custom_call_target="tpu_custom_call" | custom-call | flops 3758096384 | bytes 11010048 | tf_op jit(solution)/shard_map/forward/pallas_call | solution.py:24
  52.5 10.8 %collective-permute-done.8.refs_1_.refs_21_ = bf16[1,256,1024]{2,1,0:T(8,128)(2,1)S(1)} collective-permute-done((bf16[1,256,1024]{2,1,0:T(8,128)(2,1)S(1)}, bf16[1,256,1024]{2,1,0:T(8,128)(2,1)S(1)}, u32[]{:S(2)}, u32[]{:S(2)}) %collective-permute-start.8) | collective-permute-done | bytes 524320 | tf_op jit(solution)/shard_map/ppermute | solution.py:401
  63.3 11.6 %cut.4 = (bf16[2,512,1536]{2,1,0:T(8,128)(2,1)}, bf16[2,512,1536]{2,1,0:T(8,128)(2,1)}) custom-call(s32[5]{0:T(128)S(1)} %stack.113.ids_ref, bf16[3584,2048]{1,0:T(8,128)(2,1)} %bitcast.202, bf16[3584,512]{1,0:T(8,128)(2,1)} %bitcast.194, bf16[1,256,1024]{2,1,0:T(8,128)(2,1)S(1)} %collective-permute-done.8.refs_1_.refs_21_), custom_call_target="tpu_custom_call" | custom-call | bytes 12582912 | tf_op jit(solution)/shard_map/cut/pallas_call | solution.py:24
  101.8 42.6 %collective-permute-done.4 = f32[1,8,128]{2,1,0:T(8,128)S(1)} collective-permute-done((f32[1,8,128]{2,1,0:T(8,128)S(1)}, f32[1,8,128]{2,1,0:T(8,128)S(1)}, u32[]{:S(2)}, u32[]{:S(2)}) %collective-permute-start.4) | collective-permute-done | bytes 4128 | tf_op jit(solution)/shard_map/ppermute | solution.py:401
  153.8 42.8 %collective-permute-done.14.refs_20_ = bf16[1,256,1024]{2,1,0:T(8,128)(2,1)S(1)} collective-permute-done((bf16[1,256,1024]{2,1,0:T(8,128)(2,1)S(1)}, bf16[1,256,1024]{2,1,0:T(8,128)(2,1)S(1)}, u32[]{:S(2)}, u32[]{:S(2)}) %collective-permute-start.14) | collective-permute-done | bytes 524320 | tf_op jit(solution)/shard_map/ppermute | solution.py:401
  196.6 11.2 %collective-permute-done.16.refs_28_ = bf16[1,256,1024]{2,1,0:T(8,128)(2,1)S(1)} collective-permute-done((bf16[1,256,1024]{2,1,0:T(8,128)(2,1)S(1)}, bf16[1,256,1024]{2,1,0:T(8,128)(2,1)S(1)}, u32[]{:S(2)}, u32[]{:S(2)}) %collective-permute-start.16) | collective-permute-done | bytes 524320 | tf_op jit(solution)/shard_map/ppermute | solution.py:401
  257.5 9.5 collective-permute-start.27
  269.5 17.7 %cut.6 = (bf16[2,896,1024]{2,1,0:T(8,128)(2,1)}, bf16[2,896,1024]{2,1,0:T(8,128)(2,1)}) custom-call(s32[5]{0:T(128)S(1)} %stack.107.ids_ref, bf16[3584,2048]{1,0:T(8,128)(2,1)} %bitcast.204, bf16[2,512,1536]{2,1,0:T(8,128)(2,1)S(1)} %collective-permute-done.10.refs_0_.refs_1_.refs_3_.refs_9_.refs_11_, ...), custom_call_target="tpu_custom_call" | custom-call | bytes 14680064 | tf_op jit(solution)/shard_map/cut/pallas_call | solution.py:24
  289.4 12.2 %collective-permute-start.24 = (bf16[4,256,1536]{2,1,0:T(8,128)(2,1)}, bf16[4,256,1536]{2,1,0:T(8,128)(2,1)}, u32[]{:S(2)}, u32[]{:S(2)}) collective-permute-start(bf16[4,256,1536]{2,1,0:T(8,128)(2,1)} %pad_maximum_fusion.2), channel_id=1, source_target_pairs={{0,8},{2,10},{4,12},{6,14},{24,16},{26,18},{28,20},{30,22},{1,9},{... | collective-permute-start | bytes 9437192 | tf_op jit(solution)/shard_map/ppermute | solution.py:402
  301.6 32.4 %collective-permute-done.27.refs_4_.refs_5_.refs_6_.refs_7_.refs_12_.refs_13_.refs_14_.refs_15_ = bf16[4,256,1536]{2,1,0:T(8,128)(2,1)} collective-permute-done((bf16[4,256,1536]{2,1,0:T(8,128)(2,1)}, bf16[4,256,1536]{2,1,0:T(8,128)(2,1)}, u32[]{:S(2)}, u32[]{:S(2)}) %collective-permute-start.27) | collective-permute-done | bytes 3145760 | tf_op jit(solution)/shard_map/ppermute | solution.py:402
  358.1 35.8 %collective-permute-done.24.refs_4_.refs_5_.refs_6_.refs_7_.refs_12_.refs_13_.refs_14_.refs_15_ = bf16[4,256,1536]{2,1,0:T(8,128)(2,1)} collective-permute-done((bf16[4,256,1536]{2,1,0:T(8,128)(2,1)}, bf16[4,256,1536]{2,1,0:T(8,128)(2,1)}, u32[]{:S(2)}, u32[]{:S(2)}) %collective-permute-start.24) | collective-permute-done | bytes 3145760 | tf_op jit(solution)/shard_map/ppermute | solution.py:402
  440.8 20.3 %collective-permute-done.34 = bf16[256,1024]{1,0:T(8,128)(2,1)S(1)} collective-permute-done((bf16[256,1024]{1,0:T(8,128)(2,1)S(1)}, bf16[256,1024]{1,0:T(8,128)(2,1)S(1)}, u32[]{:S(2)}, u32[]{:S(2)}) %collective-permute-start.34) | collective-permute-done | bytes 524320 | tf_op jit(solution)/shard_map/ppermute | solution.py:402
  525.3 23.2 %collective-permute-start.48 = (bf16[4,128,1024]{2,1,0:T(8,128)(2,1)}, bf16[4,128,1024]{2,1,0:T(8,128)(2,1)}, u32[]{:S(2)}, u32[]{:S(2)}) collective-permute-start(bf16[4,128,1024]{2,1,0:T(8,128)(2,1)} %pack.18), channel_id=1, source_target_pairs={{0,8},{2,10},{4,12},{6,14},{8,0},{10,2},{12,4},{14,6},{16,24},{18,... | collective-permute-start | bytes 3145736 | tf_op jit(solution)/shard_map/ppermute | solution.py:403
  579.9 16.7 %collective-permute-start.53 = (bf16[4,128,1024]{2,1,0:T(8,128)(2,1)}, bf16[4,128,1024]{2,1,0:T(8,128)(2,1)}, u32[]{:S(2)}, u32[]{:S(2)}) collective-permute-start(bf16[4,128,1024]{2,1,0:T(8,128)(2,1)} %pack.19), channel_id=1, source_target_pairs={{0,8},{2,10},{4,12},{6,14},{8,0},{10,2},{12,4},{14,6},{16,24},{18,... | collective-permute-start | bytes 3145736 | tf_op jit(solution)/shard_map/ppermute | solution.py:403
  649.1 15.6 %collective-permute-start.58 = (bf16[4,128,1024]{2,1,0:T(8,128)(2,1)}, bf16[4,128,1024]{2,1,0:T(8,128)(2,1)S(1)}, u32[]{:S(2)}, u32[]{:S(2)}) collective-permute-start(bf16[4,128,1024]{2,1,0:T(8,128)(2,1)} %pack.21), channel_id=1, source_target_pairs={{0,8},{2,10},{4,12},{6,14},{8,0},{10,2},{12,4},{14,6},{16,24},{18,... | collective-permute-start | bytes 3145736 | tf_op jit(solution)/shard_map/ppermute | solution.py:403
  701.3 15.1 %collective-permute-start.61 = (bf16[4,128,1024]{2,1,0:T(8,128)(2,1)S(1)}, bf16[4,128,1024]{2,1,0:T(8,128)(2,1)S(1)}, u32[]{:S(2)}, u32[]{:S(2)}) collective-permute-start(bf16[4,128,1024]{2,1,0:T(8,128)(2,1)S(1)} %pack.22), channel_id=1, source_target_pairs={{0,8},{2,10},{4,12},{6,14},{8,0},{10,2},{12,4},{14,6},{16,24},{18,... | collective-permute-start | bytes 3145736 | tf_op jit(solution)/shard_map/ppermute | solution.py:403
  719.4 12.8 %collective-permute-start.57 = (bf16[4,128,1024]{2,1,0:T(8,128)(2,1)}, bf16[4,128,1024]{2,1,0:T(8,128)(2,1)S(1)}, u32[]{:S(2)}, u32[]{:S(2)}) collective-permute-start(bf16[4,128,1024]{2,1,0:T(8,128)(2,1)} %pack.20), channel_id=1, source_target_pairs={{0,8},{2,10},{4,12},{6,14},{8,0},{10,2},{12,4},{14,6},{16,24},{18,... | collective-permute-start | bytes 3145736 | tf_op jit(solution)/shard_map/ppermute | solution.py:403
  751.5 10.9 %collective-permute-done.57.refs_4_.refs_5_.refs_6_.refs_7_.refs_2_ = bf16[4,128,1024]{2,1,0:T(8,128)(2,1)S(1)} collective-permute-done((bf16[4,128,1024]{2,1,0:T(8,128)(2,1)}, bf16[4,128,1024]{2,1,0:T(8,128)(2,1)S(1)}, u32[]{:S(2)}, u32[]{:S(2)}) %collective-permute-start.57) | collective-permute-done | bytes 1048608 | tf_op jit(solution)/shard_map/ppermute | solution.py:403
  769.8 11.4 %collective-permute-start.78 = (bf16[4,128,1024]{2,1,0:T(8,128)(2,1)}, bf16[4,128,1024]{2,1,0:T(8,128)(2,1)}, u32[]{:S(2)}, u32[]{:S(2)}) collective-permute-start(bf16[4,128,1024]{2,1,0:T(8,128)(2,1)} %pack.27), channel_id=1, source_target_pairs={{0,8},{2,10},{4,12},{6,14},{8,0},{10,2},{12,4},{14,6},{16,24},{18,... | collective-permute-start | bytes 3145736 | tf_op jit(solution)/shard_map/ppermute | solution.py:403
  783.7 15.5 %collective-permute-start.74 = (bf16[4,128,1024]{2,1,0:T(8,128)(2,1)}, bf16[4,128,1024]{2,1,0:T(8,128)(2,1)}, u32[]{:S(2)}, u32[]{:S(2)}) collective-permute-start(bf16[4,128,1024]{2,1,0:T(8,128)(2,1)} %pack.25), channel_id=1, source_target_pairs={{0,8},{2,10},{4,12},{6,14},{8,0},{10,2},{12,4},{14,6},{16,24},{18,... | collective-permute-start | bytes 3145736 | tf_op jit(solution)/shard_map/ppermute | solution.py:403
  801.8 27.1 %collective-permute-start.75 = (bf16[4,128,1024]{2,1,0:T(8,128)(2,1)}, bf16[4,128,1024]{2,1,0:T(8,128)(2,1)}, u32[]{:S(2)}, u32[]{:S(2)}) collective-permute-start(bf16[4,128,1024]{2,1,0:T(8,128)(2,1)} %pack.26), channel_id=1, source_target_pairs={{0,8},{2,10},{4,12},{6,14},{8,0},{10,2},{12,4},{14,6},{16,24},{18,... | collective-permute-start | bytes 3145736 | tf_op jit(solution)/shard_map/ppermute | solution.py:403
  869.0 21.3 %collective-permute-done.79.refs_2_ = bf16[2,2,128,1024]{3,2,1,0:T(8,128)(2,1)S(1)} collective-permute-done((bf16[2,2,128,1024]{3,2,1,0:T(8,128)(2,1)}, bf16[2,2,128,1024]{3,2,1,0:T(8,128)(2,1)S(1)}, u32[]{:S(2)}, u32[]{:S(2)}) %collective-permute-start.79) | collective-permute-done | bytes 1048608 | tf_op jit(solution)/shard_map/ppermute | solution.py:401
  900.5 12.2 %collective-permute-done.76.refs_2_ = bf16[2,2,128,1024]{3,2,1,0:T(8,128)(2,1)S(1)} collective-permute-done((bf16[2,2,128,1024]{3,2,1,0:T(8,128)(2,1)}, bf16[2,2,128,1024]{3,2,1,0:T(8,128)(2,1)S(1)}, u32[]{:S(2)}, u32[]{:S(2)}) %collective-permute-start.76) | collective-permute-done | bytes 1048608 | tf_op jit(solution)/shard_map/ppermute | solution.py:401
  913.0 10.9 %collective-permute-done.72.refs_2_ = bf16[2,1,128,1024]{3,2,1,0:T(8,128)(2,1)S(1)} collective-permute-done((bf16[2,1,128,1024]{3,2,1,0:T(8,128)(2,1)S(1)}, bf16[2,1,128,1024]{3,2,1,0:T(8,128)(2,1)S(1)}, u32[]{:S(2)}, u32[]{:S(2)}) %collective-permute-start.72) | collective-permute-done | bytes 524320 | tf_op jit(solution)/shard_map/ppermute | solution.py:401
  (584 shorter events, 485.9 us)
Async XLA Ops:
  6.5 72.7 %all-reduce.2.cloned.1.call-start = ((), (), s32[]{:S(2)}) async-start(), calls=%async_computation | async-start | bytes 524288 | tf_op jit(solution)/shard_map/psum | solution.py:449
  74.9 141.8 %collective-permute-start.9 = (bf16[2,512,1536]{2,1,0:T(8,128)(2,1)}, bf16[2,512,1536]{2,1,0:T(8,128)(2,1)}, u32[]{:S(2)}, u32[]{:S(2)}) collective-permute-start(bf16[2,512,1536]{2,1,0:T(8,128)(2,1)} %get-tuple-element.51), channel_id=1, source_target_pairs={{0,4},{2,6},{4,0},{6,2},{8,12},{10,14},{12,8},{14,10},{16,20},{18,... | collective-permute-start | bytes 9437192 | tf_op jit(solution)/shard_map/ppermute | solution.py:401
  88.2 63.2 %collective-permute-start.12 = (bf16[2,128,1536]{2,1,0:T(8,128)(2,1)}, bf16[2,128,1536]{2,1,0:T(8,128)(2,1)S(1)}, u32[]{:S(2)}, u32[]{:S(2)}) collective-permute-start(bf16[2,128,1536]{2,1,0:T(8,128)(2,1)} %pad_maximum_fusion.16), channel_id=1, source_target_pairs={{0,2},{2,0},{4,6},{6,4},{8,10},{10,8},{12,14},{14,12},{16,18},{18,... | collective-permute-start | bytes 2359304 | tf_op jit(solution)/shard_map/ppermute | solution.py:401
  92.2 52.2 %collective-permute-start.4 = (f32[1,8,128]{2,1,0:T(8,128)S(1)}, f32[1,8,128]{2,1,0:T(8,128)S(1)}, u32[]{:S(2)}, u32[]{:S(2)}) collective-permute-start(f32[1,8,128]{2,1,0:T(8,128)S(1)} %fusion.19), channel_id=1, source_target_pairs={{0,4},{2,6},{4,0},{6,2},{8,12},{10,14},{12,8},{14,10},{16,20},{18,... | collective-permute-start | bytes 12296 | tf_op jit(solution)/shard_map/ppermute | solution.py:401
  148.0 72.7 %collective-permute-start.25 = (bf16[2,256,1536]{2,1,0:T(8,128)(2,1)S(1)}, bf16[2,256,1536]{2,1,0:T(8,128)(2,1)S(1)}, u32[]{:S(2)}, u32[]{:S(2)}) collective-permute-start(bf16[2,256,1536]{2,1,0:T(8,128)(2,1)S(1)} %get-tuple-element.57), channel_id=1, source_target_pairs={{0,4},{2,6},{4,0},{6,2},{8,12},{10,14},{12,8},{14,10},{16,20},{18,... | collective-permute-start | bytes 4718600 | tf_op jit(solution)/shard_map/ppermute | solution.py:401
  150.3 57.5 %collective-permute-start.16 = (bf16[1,256,1024]{2,1,0:T(8,128)(2,1)S(1)}, bf16[1,256,1024]{2,1,0:T(8,128)(2,1)S(1)}, u32[]{:S(2)}, u32[]{:S(2)}) collective-permute-start(bf16[1,256,1024]{2,1,0:T(8,128)(2,1)S(1)} %bitcast.98), channel_id=1, source_target_pairs={{0,4},{2,6},{4,0},{6,2},{8,12},{10,14},{12,8},{14,10},{16,20},{18,... | collective-permute-start | bytes 1572872 | tf_op jit(solution)/shard_map/ppermute | solution.py:401
  151.3 63.8 %collective-permute-start.19 = (bf16[1,256,1024]{2,1,0:T(8,128)(2,1)S(1)}, bf16[1,256,1024]{2,1,0:T(8,128)(2,1)S(1)}, u32[]{:S(2)}, u32[]{:S(2)}) collective-permute-start(bf16[1,256,1024]{2,1,0:T(8,128)(2,1)S(1)} %bitcast.114), channel_id=1, source_target_pairs={{0,4},{2,6},{4,0},{6,2},{8,12},{10,14},{12,8},{14,10},{16,20},{18,... | collective-permute-start | bytes 1572872 | tf_op jit(solution)/shard_map/ppermute | solution.py:401
  257.5 76.6 %collective-permute-start.27 = (bf16[4,256,1536]{2,1,0:T(8,128)(2,1)}, bf16[4,256,1536]{2,1,0:T(8,128)(2,1)}, u32[]{:S(2)}, u32[]{:S(2)}) collective-permute-start(bf16[4,256,1536]{2,1,0:T(8,128)(2,1)} %pad_maximum_fusion.3), channel_id=1, source_target_pairs={{0,8},{2,10},{4,12},{6,14},{24,16},{26,18},{28,20},{30,22},{1,9},{... | collective-permute-start | bytes 9437192 | tf_op jit(solution)/shard_map/ppermute | solution.py:402
  287.2 114.7 %collective-permute-start.22 = (bf16[2,896,1024]{2,1,0:T(8,128)(2,1)}, bf16[2,896,1024]{2,1,0:T(8,128)(2,1)}, u32[]{:S(2)}, u32[]{:S(2)}) collective-permute-start(bf16[2,896,1024]{2,1,0:T(8,128)(2,1)} %get-tuple-element.55), channel_id=1, source_target_pairs={{0,4},{2,6},{4,0},{6,2},{8,12},{10,14},{12,8},{14,10},{16,20},{18,... | collective-permute-start | bytes 11010056 | tf_op jit(solution)/shard_map/ppermute | solution.py:401
  289.4 104.6 %collective-permute-start.24 = (bf16[4,256,1536]{2,1,0:T(8,128)(2,1)}, bf16[4,256,1536]{2,1,0:T(8,128)(2,1)}, u32[]{:S(2)}, u32[]{:S(2)}) collective-permute-start(bf16[4,256,1536]{2,1,0:T(8,128)(2,1)} %pad_maximum_fusion.2), channel_id=1, source_target_pairs={{0,8},{2,10},{4,12},{6,14},{24,16},{26,18},{28,20},{30,22},{1,9},{... | collective-permute-start | bytes 9437192 | tf_op jit(solution)/shard_map/ppermute | solution.py:402
  353.0 53.3 %collective-permute-start.28 = (bf16[12,128,512]{2,1,0:T(8,128)(2,1)S(1)}, bf16[12,128,512]{2,1,0:T(8,128)(2,1)S(1)}, u32[]{:S(2)}, u32[]{:S(2)}) collective-permute-start(bf16[12,128,512]{2,1,0:T(8,128)(2,1)S(1)} %merge_partial.15.mine_ref.refs_0_), channel_id=1, source_target_pairs={{8,16},{10,18},{12,20},{14,22},{16,8},{18,10},{20,12},{22,14},{9,1... | collective-permute-start | bytes 4718600 | tf_op jit(solution)/shard_map/ppermute | solution.py:406
  405.8 104.1 %collective-permute-start.23 = (bf16[2,896,1024]{2,1,0:T(8,128)(2,1)}, bf16[2,896,1024]{2,1,0:T(8,128)(2,1)}, u32[]{:S(2)}, u32[]{:S(2)}) collective-permute-start(bf16[2,896,1024]{2,1,0:T(8,128)(2,1)} %pad_maximum_fusion), channel_id=1, source_target_pairs={{0,2},{2,0},{4,6},{6,4},{8,10},{10,8},{12,14},{14,12},{16,18},{18,... | collective-permute-start | bytes 11010056 | tf_op jit(solution)/shard_map/ppermute | solution.py:401
  409.4 65.1 %collective-permute-start.41 = (bf16[4,128,1536]{2,1,0:T(8,128)(2,1)}, bf16[4,128,1536]{2,1,0:T(8,128)(2,1)}, u32[]{:S(2)}, u32[]{:S(2)}) collective-permute-start(bf16[4,128,1536]{2,1,0:T(8,128)(2,1)} %pack.15), channel_id=1, source_target_pairs={{0,8},{2,10},{4,12},{6,14},{8,0},{10,2},{12,4},{14,6},{16,24},{18,... | collective-permute-start | bytes 4718600 | tf_op jit(solution)/shard_map/ppermute | solution.py:403
  440.8 64.7 %collective-permute-start.45 = (bf16[4,128,1536]{2,1,0:T(8,128)(2,1)}, bf16[4,128,1536]{2,1,0:T(8,128)(2,1)}, u32[]{:S(2)}, u32[]{:S(2)}) collective-permute-start(bf16[4,128,1536]{2,1,0:T(8,128)(2,1)} %pack.16), channel_id=1, source_target_pairs={{0,8},{2,10},{4,12},{6,14},{8,0},{10,2},{12,4},{14,6},{16,24},{18,... | collective-permute-start | bytes 4718600 | tf_op jit(solution)/shard_map/ppermute | solution.py:403
  489.1 66.9 %collective-permute-start.36 = (bf16[4,256,1024]{2,1,0:T(8,128)(2,1)}, bf16[4,256,1024]{2,1,0:T(8,128)(2,1)}, u32[]{:S(2)}, u32[]{:S(2)}) collective-permute-start(bf16[4,256,1024]{2,1,0:T(8,128)(2,1)} %pad_maximum_fusion.6), channel_id=1, source_target_pairs={{0,2},{2,0},{4,6},{6,4},{8,10},{10,8},{12,14},{14,12},{16,18},{18,... | collective-permute-start | bytes 6291464 | tf_op jit(solution)/shard_map/ppermute | solution.py:401
  505.5 59.3 %collective-permute-start.40 = (bf16[4,256,1024]{2,1,0:T(8,128)(2,1)}, bf16[4,256,1024]{2,1,0:T(8,128)(2,1)}, u32[]{:S(2)}, u32[]{:S(2)}) collective-permute-start(bf16[4,256,1024]{2,1,0:T(8,128)(2,1)} %pad_maximum_fusion.7), channel_id=1, source_target_pairs={{0,2},{2,0},{4,6},{6,4},{8,10},{10,8},{12,14},{14,12},{16,18},{18,... | collective-permute-start | bytes 6291464 | tf_op jit(solution)/shard_map/ppermute | solution.py:401
  512.8 52.0 %collective-permute-start.30 = (bf16[4,128,1024]{2,1,0:T(8,128)(2,1)}, bf16[4,128,1024]{2,1,0:T(8,128)(2,1)}, u32[]{:S(2)}, u32[]{:S(2)}) collective-permute-start(bf16[4,128,1024]{2,1,0:T(8,128)(2,1)} %pack.14), channel_id=1, source_target_pairs={{0,8},{2,10},{4,12},{6,14},{8,0},{10,2},{12,4},{14,6},{16,24},{18,... | collective-permute-start | bytes 3145736 | tf_op jit(solution)/shard_map/ppermute | solution.py:403
  568.8 56.4 %collective-permute-start.46 = (bf16[12,128,512]{2,1,0:T(8,128)(2,1)}, bf16[12,128,512]{2,1,0:T(8,128)(2,1)}, u32[]{:S(2)}, u32[]{:S(2)}) collective-permute-start(bf16[12,128,512]{2,1,0:T(8,128)(2,1)} %merge_partial.20.mine_ref.refs_3_), channel_id=1, source_target_pairs={{8,16},{10,18},{12,20},{14,22},{16,8},{18,10},{20,12},{22,14},{9,1... | collective-permute-start | bytes 4718600 | tf_op jit(solution)/shard_map/ppermute | solution.py:406
  579.9 61.4 %collective-permute-start.53 = (bf16[4,128,1024]{2,1,0:T(8,128)(2,1)}, bf16[4,128,1024]{2,1,0:T(8,128)(2,1)}, u32[]{:S(2)}, u32[]{:S(2)}) collective-permute-start(bf16[4,128,1024]{2,1,0:T(8,128)(2,1)} %pack.19), channel_id=1, source_target_pairs={{0,8},{2,10},{4,12},{6,14},{8,0},{10,2},{12,4},{14,6},{16,24},{18,... | collective-permute-start | bytes 3145736 | tf_op jit(solution)/shard_map/ppermute | solution.py:403
  692.6 53.5 %collective-permute-start.60 = (bf16[12,128,512]{2,1,0:T(8,128)(2,1)}, bf16[12,128,512]{2,1,0:T(8,128)(2,1)S(1)}, u32[]{:S(2)}, u32[]{:S(2)}) collective-permute-start(bf16[12,128,512]{2,1,0:T(8,128)(2,1)} %merge_partial.25.mine_ref.refs_3_), channel_id=1, source_target_pairs={{8,16},{10,18},{12,20},{14,22},{16,8},{18,10},{20,12},{22,14},{9,1... | collective-permute-start | bytes 4718600 | tf_op jit(solution)/shard_map/ppermute | solution.py:406
  769.8 71.7 %collective-permute-start.78 = (bf16[4,128,1024]{2,1,0:T(8,128)(2,1)}, bf16[4,128,1024]{2,1,0:T(8,128)(2,1)}, u32[]{:S(2)}, u32[]{:S(2)}) collective-permute-start(bf16[4,128,1024]{2,1,0:T(8,128)(2,1)} %pack.27), channel_id=1, source_target_pairs={{0,8},{2,10},{4,12},{6,14},{8,0},{10,2},{12,4},{14,6},{16,24},{18,... | collective-permute-start | bytes 3145736 | tf_op jit(solution)/shard_map/ppermute | solution.py:403
  783.7 75.0 %collective-permute-start.74 = (bf16[4,128,1024]{2,1,0:T(8,128)(2,1)}, bf16[4,128,1024]{2,1,0:T(8,128)(2,1)}, u32[]{:S(2)}, u32[]{:S(2)}) collective-permute-start(bf16[4,128,1024]{2,1,0:T(8,128)(2,1)} %pack.25), channel_id=1, source_target_pairs={{0,8},{2,10},{4,12},{6,14},{8,0},{10,2},{12,4},{14,6},{16,24},{18,... | collective-permute-start | bytes 3145736 | tf_op jit(solution)/shard_map/ppermute | solution.py:403
  801.8 57.1 %collective-permute-start.75 = (bf16[4,128,1024]{2,1,0:T(8,128)(2,1)}, bf16[4,128,1024]{2,1,0:T(8,128)(2,1)}, u32[]{:S(2)}, u32[]{:S(2)}) collective-permute-start(bf16[4,128,1024]{2,1,0:T(8,128)(2,1)} %pack.26), channel_id=1, source_target_pairs={{0,8},{2,10},{4,12},{6,14},{8,0},{10,2},{12,4},{14,6},{16,24},{18,... | collective-permute-start | bytes 3145736 | tf_op jit(solution)/shard_map/ppermute | solution.py:403
  869.0 61.3 %collective-permute-start.82 = (bf16[2,2,128,1024]{3,2,1,0:T(8,128)(2,1)}, bf16[2,2,128,1024]{3,2,1,0:T(8,128)(2,1)S(1)}, u32[]{:S(2)}, u32[]{:S(2)}) collective-permute-start(bf16[2,2,128,1024]{3,2,1,0:T(8,128)(2,1)} %pad_maximum_fusion.15), channel_id=1, source_target_pairs={{0,2},{2,0},{4,6},{6,4},{8,10},{10,8},{12,14},{14,12},{16,18},{18,... | collective-permute-start | bytes 3145736 | tf_op jit(solution)/shard_map/ppermute | solution.py:401
  (198 other events, 4427.6 us)
Sparse Core Ops, SparseCore 0:
  51.7 27.4 all-reduce.1

commit v2 on v1

--- a/solution.py
+++ b/solution.py
@@ -11,7 +11,7 @@
 EPS = 1e-06
 FLOOR = 0.1
 LAYERS = 4
-LEAD = 5
+LEAD = 7
 VMEM = 48 * 1024 * 1024
 F32 = jnp.float32
 BF16 = jnp.bfloat16
@@ -36,6 +36,19 @@
         cost_estimate=pl.CostEstimate(flops=cost[0], bytes_accessed=cost[1], transcendentals=0),
         name=name,
     )(*prefetch, *operands)
+
+
+def gate(value, after):
+    anywhere = pl.BlockSpec(memory_space=pl.ANY)
+    return pl.pallas_call(
+        lambda *refs: None,
+        out_shape=jax.ShapeDtypeStruct(value.shape, value.dtype),
+        in_specs=[anywhere] * (1 + len(after)),
+        out_specs=anywhere,
+        input_output_aliases={0: 0},
+        cost_estimate=pl.CostEstimate(flops=1, bytes_accessed=1, transcendentals=0),
+        name="gate",
+    )(value, *after)
 
 
 def merge_kernel(peers, parts, final, extra, ids_ref, scale_ref, *refs):
@@ -164,11 +177,11 @@
 
         @pl.when(ids_ref[HUB] == 0)
         def _():
-            for peer, ref in enumerate(refs[:-1]):
-                out_ref[peer] = ref[...]
-
-
-def pack_step(ids, mine, other, source, row, rows, half, peers):
+            for peer in range(up):
+                out_ref[peer] = refs[peer][...]
+
+
+def pack_step(ids, mine, other, source, row, rows, half, peers, after):
     in_specs = [planes_spec(mine, rows, half), planes_spec(other, rows, half)]
     operands = [mine, other]
     width = 2 * half
@@ -177,8 +190,10 @@
         in_specs.append(pl.BlockSpec((None, rows, width), lambda g, ids, i=index: (i, row, 0)))
         operands.append(array)
     shape = (max(peers, CLUSTERS), rows, width)
+    in_specs += [pl.BlockSpec(memory_space=pl.ANY)] * len(after)
+    operands += after
     return call(
-        functools.partial(pack_kernel, bool(source)),
+        functools.partial(pack_kernel, len(source)),
         (1,),
         ids,
         None,
@@ -217,13 +232,15 @@
                 out_ref[to, index] = leaf_ref[cluster, :, base:]
 
 
-def pick_step(ids, group, rows, half, peers):
+def pick_step(ids, group, rows, half, peers, after):
     in_specs, operands = [], []
     for mine, other, leaf in group:
         operands += [mine, other, leaf]
         in_specs += [planes_spec(mine, rows, half), planes_spec(other, rows, half)]
         in_specs.append(pl.BlockSpec(leaf.shape, lambda *_: (0, 0, 0)))
     shape = (peers // 2, len(group), rows, 2 * half)
+    in_specs += [pl.BlockSpec(memory_space=pl.ANY)] * len(after)
+    operands += after
     return call(
         functools.partial(pick_kernel, peers, len(group)),
         (1,),
@@ -248,7 +265,7 @@
             out_ref[...] = refs[peer][...]
 
 
-def place_step(ids, blocks, result):
+def place_step(ids, blocks, result, shape, after):
     peers = len(blocks)
     _, chunks, rows, width = blocks[0][0].shape
     step = 1 + peers
@@ -261,42 +278,40 @@
         (chunks, peers),
         ids,
         None,
-        in_specs + [pl.BlockSpec(memory_space=pl.ANY)],
-        [array for array, _ in blocks] + [result],
+        in_specs + [pl.BlockSpec(memory_space=pl.ANY)] * (len(after) + (result is not None)),
+        [array for array, _ in blocks] + [result] * (result is not None) + after,
         [
             pl.BlockSpec((rows, width), lambda c, p, ids: (ids[c * step + 1 + p], ids[c * step])),
             pl.BlockSpec((8, 128), lambda c, p, ids: (0, 0)),
         ],
-        [jax.ShapeDtypeStruct(result.shape, BF16), jax.ShapeDtypeStruct((8, 128), F32)],
+        [jax.ShapeDtypeStruct(shape, BF16), jax.ShapeDtypeStruct((8, 128), F32)],
         "place",
         (0, 4 * chunks * peers * rows * width),
-        aliases={peers: 0},
-    )
-
-
-def forward_kernel(own, batches, ids_ref, hidden_ref, weight_ref, target_ref, *outs):
+        aliases={peers: 0} if result is not None else {},
+    )
+
+
+def forward_kernel(own, batches, ids_ref, hidden_ref, weight_ref, target_ref, *refs):
+    outs = refs[-1:] if own else refs[-2:]
     total = jnp.dot(hidden_ref[...], weight_ref[...], preferred_element_type=F32)
     tokens = hidden_ref.shape[0] // batches
     span = target_ref.shape[1]
-    half = batches // 2
-    for part in range(2):
-        out_ref = outs[part]
-        out_ref[...] = total[part * half * tokens : (part + 1) * half * tokens]
-        for batch in range(half):
-            rows = pl.ds(pl.multiple_of(batch * tokens + ids_ref[0] * span, 8), span)
-            out_ref[rows, :] = out_ref[rows, :] - target_ref[part * half + batch].astype(F32)
-    if own:
+    outs[0][...] = total
+    for batch in range(batches):
+        rows = pl.ds(pl.multiple_of(batch * tokens + ids_ref[0] * span, 8), span)
+        outs[0][rows, :] = outs[0][rows, :] - target_ref[batch].astype(F32)
+    if not own:
 
         @pl.when(pl.program_id(0) == 0)
         def _():
             for batch in range(batches):
                 rows = hidden_ref[batch * tokens : (batch + 1) * tokens, :]
-                outs[2][batch] = lax.dot_general(
+                outs[1][batch] = lax.dot_general(
                     rows, rows, (((1,), (1,)), ((), ())), preferred_element_type=F32
                 )
 
 
-def forward_step(ids, flat, weight, target, block, shards, own):
+def forward_step(ids, flat, weight, target, block, shards, own, after=()):
     every, depth = flat.shape
     batches = target.shape[0]
     tokens = every // batches
@@ -304,9 +319,9 @@
     tiles = block // width
     count = tiles if own else tiles * (shards - 1)
     columns = lambda g, ids: ids[1 + g // tiles] * tiles + g % tiles
-    out_specs = [pl.BlockSpec((every // 2, width), lambda g, ids: (0, g))] * 2
-    out_shape = [jax.ShapeDtypeStruct((every // 2, count * width), F32)] * 2
-    if own:
+    out_specs = [pl.BlockSpec((every, width), lambda g, ids: (0, g))]
+    out_shape = [jax.ShapeDtypeStruct((every, count * width), F32)]
+    if not own:
         out_specs.append(pl.BlockSpec((batches, tokens, tokens), lambda g, ids: (0, 0, 0)))
         out_shape.append(jax.ShapeDtypeStruct((batches, tokens, tokens), F32))
     return call(
@@ -318,12 +333,46 @@
             pl.BlockSpec((every, depth), lambda g, ids: (0, 0)),
             pl.BlockSpec((depth, width), lambda g, ids: (0, columns(g, ids))),
             pl.BlockSpec((batches, target.shape[1], width), lambda g, ids: (0, 0, columns(g, ids))),
-        ],
-        [flat, weight, target],
+        ]
+        + [pl.BlockSpec(memory_space=pl.ANY)] * len(after),
+        [flat, weight, target, *after],
         out_specs,
         out_shape,
         "forward",
-        (2 * every * depth * count * width, 2 * depth * (every + count * width)),
+        (1, 1),
+    )
+
+
+def grad_kernel(batches, ids_ref, token_ref, gram_ref, mine_ref, *refs):
+    grad_ref, total_ref = refs[-2:]
+    total = mine_ref[...]
+    for ref in refs[:-2]:
+        total = total + ref[...]
+    grad_ref[...] = (token_ref[...] * total).astype(BF16)
+    tokens = grad_ref.shape[0] // batches
+    squares = 0.0
+    for batch in range(batches):
+        rows = grad_ref[batch * tokens : (batch + 1) * tokens, :]
+        gram = lax.dot_general(rows, rows, (((1,), (1,)), ((), ())), preferred_element_type=F32)
+        squares = squares + jnp.sum(gram_ref[batch] * gram)
+    total_ref[...] = jnp.full(total_ref.shape, squares, F32)
+
+
+def grad_step(ids, token_weight, hidden_gram, mine, others):
+    arrays = [token_weight, hidden_gram, mine, *others]
+    whole = lambda a: pl.BlockSpec(a.shape, lambda *_: (0,) * a.ndim)
+    outs = [jax.ShapeDtypeStruct(mine.shape, BF16), jax.ShapeDtypeStruct((8, 128), F32)]
+    return call(
+        functools.partial(grad_kernel, hidden_gram.shape[0]),
+        (1,),
+        ids.astype(jnp.int32),
+        None,
+        [whole(a) for a in arrays],
+        arrays,
+        [whole(a) for a in outs],
+        outs,
+        "grad",
+        (1, 1),
     )
 
 
@@ -365,7 +414,7 @@
         ],
         [jax.ShapeDtypeStruct(shape, BF16)] * 2,
         "cut",
-        (0, 8 * count * shape[1] * shape[2]),
+        (1, 1),
     )
 
 
@@ -407,9 +456,8 @@
     ahead = lambda j: [(s, (s + j) % shards) for s in range(shards)]
     behind = lambda j: [(s, (s - j) % shards) for s in range(shards)]
 
-    def exchange(held):
+    def exchange(held, after=(), bit=peers // 2):
         held = list(held)
-        bit = peers // 2
         while bit:
             moved = [k for k in range(peers) if k & bit]
             arrays = {id(held[k][0]) for k in moved}
@@ -418,72 +466,103 @@
             else:
                 array = jnp.stack([held[k][0][held[k][1]] for k in moved])
             got = to_peer(array, bit)
+            if after and bit == peers // 2:
+                got = gate(got, after)
             for i, k in enumerate(moved):
                 held[k] = (got, i)
             bit //= 2
         return held
 
-    def gather_peers(arrays):
-        held = [{0: (array[None], 0)} for array in arrays]
-        bit = peers // 2
+    def gather_pair(near, distant, after, last=()):
+        top = peers // 2
+        near_top = to_peer(near[None], top)
+        distant = gate(distant, [near_top, *after])
+        distant_top = to_peer(distant[None], top)
+        distant_top = gate(distant_top, last) if last else distant_top
+        held = [
+            {0: (near[None], 0), top: (near_top, 0)},
+            {0: (distant[None], 0), top: (distant_top, 0)},
+        ]
+        bit = top // 2
         while bit:
-            keys = [(n, k) for n in range(len(held)) for k in held[n]]
-            if bit == peers // 2:
-                for n, k in keys:
-                    array, i = held[n][k]
-                    held[n][k ^ bit] = (to_peer(array[i][None], bit), 0)
-            else:
-                got = to_peer(jnp.stack([held[n][k][0][held[n][k][1]] for n, k in keys]), bit)
-                for i, (n, k) in enumerate(keys):
-                    held[n][k ^ bit] = (got, i)
+            keys = [(n, k) for n in range(2) for k in held[n]]
+            stack = jnp.stack([held[n][k][0][held[n][k][1]] for n, k in keys])
+            got = to_peer(stack, bit)
+            for i, (n, k) in enumerate(keys):
+                held[n][k] = (stack, i)
+                held[n][k ^ bit] = (got, i)
             bit //= 2
-        return [[h[k] for k in range(peers)] for h in held]
+        slots = [h[k] for h in held for k in range(peers)]
+        return slots, near_top, distant_top, stack, got
 
     local_weight = weight[0]
     flat = hidden[0].reshape(every, depth)
     turned = flat.T
     others_at = jnp.concatenate([shard[None], (shard + jnp.arange(1, shards)) % shards])
-    others = forward_step(others_at, flat, local_weight, target[0], block, shards, False)
+    others, hidden_gram = forward_step(others_at, flat, local_weight, target[0], block, shards, False)
+    own_gram = hidden_gram
+    for j in range(1, shards):
+        hidden_gram = hidden_gram + lax.ppermute(own_gram, "mp", ahead(j))
+
+    def cut_for(j, low, high, after):
+        order = [place ^ (k + peers // 2) % peers for k in range(peers)]
+        at = jnp.stack([(shard + j) % shards] + [q * pieces + low for q in order]).astype(jnp.int32)
+        return tuple(
+            cut_step(at, local_weight, None if j else turned, size, high - low, block, peers, after)
+        )
+
+    def spread(j, low, high, after, later=()):
+        hi, lo = after if type(after) is tuple else cut_for(j, low, high, after)
+        parts = peers // 2
+        held = exchange([((lo, hi)[k // parts], k % parts) for k in range(peers)], later)
+        numbers = [j * pieces + r for r in range(low, high)]
+        for i, c in enumerate(numbers):
+            own[c] = (held, i)
+        return held[parts][0], held[-1][0], hi
+
+    def lift(c, after=()):
+        held, row = own[c]
+        array = jnp.stack([a[i, row * size : (row + 1) * size] for a, i in held])
+        array = gate(array, after) if after else array
+        lifts[c] = array, leaf_to_hub(array)
+        far[c] = ([(lifts[c][1], k) for k in range(peers)], 0)
+
+    lifts = {}
+    own, far = {}, {}
+    fine = pieces >= 7
+    early = [spread(0, 0, 1 if fine else pieces, [others])]
+    if fine:
+        early.append(spread(0, 1, 2, [early[0][2]]))
     mine_at = jnp.stack([shard, shard])
-    *mine, hidden_gram = forward_step(mine_at, flat, local_weight, target[0], block, shards, True)
-    hidden_gram = lax.psum(hidden_gram, "mp")
+    (mine,) = forward_step(
+        mine_at, flat, local_weight, target[0], block, shards, True, [e[2] for e in early]
+    )
     token_weight = jnp.where(jnp.any(routes[0] == 0, axis=-1), router_prob[0], 0.0)
     token_weight = jnp.stack(
         [token_weight] + [lax.ppermute(token_weight, "mp", behind(j)) for j in range(1, shards)]
     )
     token_weight = token_weight[(jnp.arange(shards) - shard) % shards]
     token_weight = token_weight.transpose(1, 0, 2).reshape(every, 1)
-    grad_parts = []
-    for part in range(2):
-        total = mine[part]
-        for j in range(1, shards):
-            total = total + lax.ppermute(
-                others[part][:, (j - 1) * block : j * block], "mp", ahead(j)
-            )
-        grad = token_weight[part * every // 2 : (part + 1) * every // 2] * total
-        grad_parts.append(grad.astype(BF16))
-
-    def spread_grads(parts):
-        many = [gather_peers([part, leaf_to_hub(part)]) for part in parts]
-        return [[many[p][side][k] for p in range(len(parts))] for side in range(2) for k in range(peers)]
-
-    grads = {0: spread_grads(grad_parts)}
-
-    gram = sum(
-        jnp.sum(
-            hidden_gram[part * batches // 2 : (part + 1) * batches // 2]
-            * jnp.einsum(
-                "btd,bsd->bts", *[g.reshape(batches // 2, tokens, block)] * 2, preferred_element_type=F32
-            )
-        )
-        for part, g in enumerate(grad_parts)
-    )
-    gram = jnp.full((8, 128), gram)
-    total = gram
+    arrived = [
+        lax.ppermute(others[:, (j - 1) * block : j * block], "mp", ahead(j)) for j in range(1, shards)
+    ]
+    grad, squares = grad_step(
+        mine_at, token_weight, hidden_gram, gate(mine, [early[-1][0]]), arrived
+    )
+    total = squares
     for j in range(1, shards):
-        total = total + lax.ppermute(gram, "mp", ahead(j))
-    totals = [a[i, 0, 0] for side in gather_peers([total, leaf_to_hub(total)]) for a, i in side]
-    scales = 1.0 / (jnp.stack(totals) / (depth * shards * width) + EPS)
+        total = total + lax.ppermute(squares, "mp", ahead(j))
+    leaf_total = leaf_to_hub(total)
+    totals, *scalar_steps = gather_pair(total, leaf_total, [])
+    totals = jnp.stack([a[i, 0, 0] for a, i in totals])
+    scales = 1.0 / (totals / (depth * shards * width) + EPS)
+    leaf_grad = leaf_to_hub(grad)
+    lift(0, [leaf_grad, leaf_total])
+    grad_slots, *grad_steps = gather_pair(
+        grad, leaf_grad, [scalar_steps[1], early[0][1], early[-1][1]], [lifts[0][1]]
+    )
+
+    grads = {0: [[slot] for slot in grad_slots]}
 
     cluster_of = assign[:, 0].astype(jnp.int32)
     slot_clients = jnp.concatenate(
@@ -491,34 +570,25 @@
     )
     slot_clusters = cluster_of[slot_clients]
 
-    own, far = {}, {}
-
-    def spread(j, low, high, after):
-        order = [place ^ (k + peers // 2) % peers for k in range(peers)]
-        at = jnp.stack([(shard + j) % shards] + [q * pieces + low for q in order]).astype(jnp.int32)
-        hi, lo = cut_step(
-            at, local_weight, None if j else turned, size, high - low, block, peers, after
-        )
-        parts = peers // 2
-        held = exchange([((lo, hi)[k // parts], k % parts) for k in range(peers)])
-        numbers = [j * pieces + r for r in range(low, high)]
-        for i, c in enumerate(numbers):
-            own[c] = (held, i)
-        early = sum(c < lead for c in numbers)
-        if early:
-            array = leaf_to_hub(jnp.stack([a[i, : early * size] for a, i in held]))
-            for i in range(early):
-                far[numbers[i]] = ([(array, k) for k in range(peers)], i)
-        return held[-1][0]
-
-    if pieces > 3:
-        spread(0, 0, 1, [])
-        spread(0, 1, 3, [others[0]])
-        last = spread(0, 3, pieces, [grads[0][peers // 2][1][0]])
+    before = {t: [] for t in range(count)}
+
+    def column_grads(j, first_after, second_after):
+        first, second = grad_steps[2:]
+        come = lax.ppermute(gate(first, first_after), "mp", behind(j))
+        ready = gate(second, [come, *second_after])
+        pair = come, lax.ppermute(ready, "mp", behind(j))
+        grads[j] = [[(pair[0] if a is first else pair[1], i)] for a, i in grad_slots]
+        return come, ready
+
+    if fine:
+        lift(1, [lifts[0][1]])
+        before[0].append(lifts[1][0])
     else:
-        last = spread(0, 0, pieces, [])
+        last = early[0]
         for j in range(1, shards):
-            last = spread(j, 0, pieces, [last])
+            last = spread(j, 0, pieces, [last[1]])
+        for c in range(1, lead):
+            lift(c)
 
     def ids_for(c, side):
         head = [is_hub, upper, (shard + chunks[c][0]) % shards, side]
@@ -537,62 +607,118 @@
             ids_for(c, side), scales, chunk, grads[j], size, half, got, planes, held, after
         )
 
-    result = jnp.zeros((depth, width), BF16)
-    sent, got, leaf, tokens_of = {}, {}, {}, {}
+    result, chain = None, None
+    sent, got, leaf = {}, {}, {}
+    picked, turned_ones = [], []
     waiting = []
 
-    def finish(c):
-        nonlocal result, waiting
+    def pack(c):
+        nonlocal chain
         later = c + lead
         source, row = own[later] if later < count else ([], 0)
         packed = pack_step(
-            ids_for(c, upper), sent[c + 2], got[c + 2], source, row, size, half, peers
+            ids_for(c, upper), sent[c + 2], got[c + 2], source, row, size, half, peers, [chain]
         )
+        chain = packed
         leaf[c] = leaf_and_hub(packed)
         if later < count:
             far[later] = ([(leaf[c], k) for k in range(peers)], 0)
         waiting.append(c)
-        if len(waiting) == 2 or c >= count - 2:
-            lo, hi = pick_step(
-                ids_for(c, upper),
-                [(sent[w + 2], got[w + 2], leaf[w]) for w in waiting],
-                size,
-                half,
-                peers,
-            )
-            parts = peers // 2
-            held = exchange([((lo, hi)[k // parts], k % parts) for k in range(peers)])
-            where = []
-            for w in waiting:
-                where.append(((shard + chunks[w][0]) % shards)[None])
-                where.append(ranks * pieces + chunks[w][1])
-            result, token = place_step(jnp.concatenate(where).astype(jnp.int32), held, result)
-            for w in waiting:
-                tokens_of[w] = token
-            waiting = []
+
+    def pick(step):
+        nonlocal chain
+        lo, hi = pick_step(
+            ids_for(waiting[0], upper),
+            [(sent[w + 2], got[w + 2], leaf[w]) for w in waiting],
+            size,
+            half,
+            peers,
+            [chain],
+        )
+        chain = lo
+        parts = peers // 2
+        come = to_peer(hi, parts)
+        held = [(lo, k) for k in range(parts)] + [(come, k) for k in range(parts)]
+        picked.append((step, list(waiting), held))
+        waiting.clear()
+
+    def turn():
+        step, group, held = picked.pop(0)
+        come = gate(held[-1][0], [chain])
+        held = held[: peers // 2] + [(come, i) for _, i in held[peers // 2 :]]
+        turned_ones.append((step, group, exchange(held, bit=peers // 4)))
+
+    def put():
+        nonlocal result, chain
+        _, group, held = turned_ones.pop(0)
+        where = []
+        for w in group:
+            where.append(((shard + chunks[w][0]) % shards)[None])
+            where.append(ranks * pieces + chunks[w][1])
+        result, chain = place_step(
+            jnp.concatenate(where).astype(jnp.int32), held, result, (depth, width), [chain]
+        )
 
     for t in range(count + 2):
-        if t >= 3:
-            finish(t - 3)
         planes = (2 if t < count else 0) * CLUSTERS + (CLUSTERS if t >= 2 else 0)
         buffer = None
         if t >= 2:
-            buffer = merge(t - 2, 1 - upper, got[t - 2], planes, None)
+            buffer = merge(t - 2, 1 - upper, got[t - 2], planes, None, [chain])
         if t < count:
-            after = []
-            if t - 6 in leaf:
-                after.append(leaf[t - 6])
-            if t - 8 in tokens_of:
-                after.append(tokens_of[t - 8])
-            buffer = merge(t, upper, None, planes, buffer, after)
-        sent[t] = buffer
+            buffer = merge(t, upper, None, planes, buffer, before[t])
+        chain = sent[t] = buffer
         got[t] = hub_to_hub(buffer)
-        j = 1 + t * (shards - 1) // max(1, pieces * (shards - 1))
-        if t % pieces == 0 and j < shards and pieces > 3:
-            last = spread(j, 0, pieces, [last, got[t]])
-        if t % pieces == min(2, pieces - 1) and j < shards:
-            grads[j] = spread_grads([lax.ppermute(g, "mp", behind(j)) for g in grad_parts])
-    finish(count - 1)
+        if len(waiting) == 2:
+            pick(t)
+        if t >= 4:
+            pack(t - 4)
+        if turned_ones and turned_ones[0][0] <= t - 2:
+            put()
+        if picked and picked[0][0] <= t - 1:
+            turn()
+        j, step = t // pieces + 1, t % pieces
+        if not fine:
+            if j < shards:
+                column_grads(j, [got[t]], [])
+            continue
+        if t == 0:
+            pair = spread(0, 2, 4, [grad_steps[1]], [sent[0]])
+            rest_cut = cut_for(0, 4, pieces, [pair[0]])
+            before[1].append(rest_cut[0])
+        if t == 2:
+            rest = spread(0, 4, pieces, rest_cut, [sent[2]])
+            cuts = cut_for(1, 0, 2, [rest[0]])
+            before[3].append(cuts[0])
+        if t == 3:
+            for array, step in zip(column_grads(1, [sent[0]], [sent[3]]), (4, 5)):
+                before[step].append(array)
+        if t in (3, 5, 7):
+            low, high = {3: (0, 2), 5: (2, 5), 7: (5, pieces)}[t]
+            before[t + 1].append(spread(1, low, high, cuts, [sent[t]])[0])
+        if t in (4, 6):
+            cuts = cut_for(1, *{4: (2, 5), 6: (5, pieces)}[t], [sent[t]])
+            before[t + 1].append(cuts[0])
+        if t + 2 < lead:
+            lift(t + 2, [lifts[t + 1][1], sent[t]])
+            before[t + 1].append(lifts[t + 2][0])
+    pack(count - 2)
+    pack(count - 1)
+    later = waiting[-2:]
+    del waiting[-2:]
+    if waiting:
+        pick(count + 2)
+    while turned_ones:
+        put()
+    for w in later:
+        waiting.append(w)
+        pick(count + 2)
+        turn()
+        if turned_ones:
+            put()
+    while picked or turned_ones:
+        if picked:
+            turn()
+        put()
     return result[None]
 
 

time: 969 us -> 916 us (0.945)
  starting transfers between devices: 258 us -> 201 us
  local copies, waits for them, and re-layouts: 80.6 us -> 101 us
  between operations: 16.8 us -> 2.28 us
  Pallas kernels: 259 us -> 271 us
    ppermute x39 -> x36, waiting for transfers between devices: 181 us -> 66.5 us  [body(): to_peer = lambda array, k: lax.ppermute(array, 'client', swap(k))]
    ppermute x14, waiting for transfers between devices: 20.3 us -> 127 us  [body(): lax.ppermute(array, 'client', between([(0, 1), (1, 0), (2, 3), (3, 2)]))]
    ppermute x14, starting transfers between devices: 160 us -> 81.5 us  [body(): lax.ppermute(array, 'client', between([(0, 1), (1, 0), (2, 3), (3, 2)]))]
    ppermute x1, waiting for transfers between devices: 0.01 us -> 20.3 us  [body(): lax.ppermute(token_weight, 'mp', behind(j))]
    slice x20 -> x26, local copies, waits for them, and re-layouts: 6.55 us -> 23.2 us  [exchange(): array = jnp.stack([held[k][0][held[k][1]] for k in moved])]
    ppermute x8 -> x9, waiting for transfers between devices: 98 us -> 85.1 us  [body(): lax.ppermute(array, 'client', between([(0, 1), (3, 2)]))]
    pallas_call x64 -> x68, Pallas kernels: 259 us -> 271 us  [call(): pl.pallas_call(kernel, out_shape=out_shape, grid_spec=pltpu.PrefetchScala...]
    ppermute x39 -> x36, starting transfers between devices: 19.5 us -> 27.8 us  [body(): to_peer = lambda array, k: lax.ppermute(array, 'client', swap(k))]
  transfers between devices with their start and end apart: 84 -> 81, of which waited for: 26 -> 28; matrix products, arithmetic and copies ran while one was open for 7% -> 9% of each run, Pallas kernels for 27% -> 29%
where the time goes in v2:
time: 916 us; the launch traced here: 905 us
  waiting for transfers between devices  299 us (33%)
  Pallas kernels  271 us (30%)
  starting transfers between devices  201 us (22%)
  local copies, waits for them, and re-layouts  101 us (11%)
  other arithmetic  31.6 us (3%)
    pallas_call x68, Pallas kernels, call(): pl.pallas_call(kernel, out_shape=out_shape, grid_spec=pltpu.PrefetchScala...  271 us
    ppermute x14, waiting for transfers between devices, body(): lax.ppermute(array, 'client', between([(0, 1), (1, 0), (2, 3), (3, 2)]))  127 us
    ppermute x9, waiting for transfers between devices, body(): lax.ppermute(array, 'client', between([(0, 1), (3, 2)]))  85.1 us
    ppermute x14, starting transfers between devices, body(): lax.ppermute(array, 'client', between([(0, 1), (1, 0), (2, 3), (3, 2)]))  81.5 us
    ppermute x36, waiting for transfers between devices, body(): to_peer = lambda array, k: lax.ppermute(array, 'client', swap(k))  66.5 us
    ppermute x9, starting transfers between devices, body(): lax.ppermute(array, 'client', between([(0, 1), (3, 2)]))  54.8 us
    unnamed x318, local copies, waits for them, and re-layouts  46.7 us
    ppermute x36, starting transfers between devices, body(): to_peer = lambda array, k: lax.ppermute(array, 'client', swap(k))  27.8 us
  transfers between devices with their start and end apart: 81, of which 28 were waited for; matrix products, arithmetic and copies ran while one was open for 9% of the time, Pallas kernels for 29%

profile of v2, /device:TPU:0, one launch (start us, length us, event | category | flops | bytes accessed | tf_op | source)
XLA Modules:
  0.0 905.2 jit_solution(4130720341829410425)
XLA Ops:
  1.3 10.4 %forward.2 = (f32[512,1024]{1,0:T(8,128)}, f32[4,128,128]{2,1,0:T(8,128)S(1)}) custom-call(s32[2]{0:T(128)S(1)} %pad_add_fusion.2.ids_ref, bf16[512,3584]{1,0:T(8,128)(2,1)} %bitcast.76, bf16[3584,2048]{1,0:T(8,128)(2,1)} %bitcast.67, bf16[4,64,2048]{2,1,0:T(8,128)(2,1)S(1)} %bitcast.63), custom_call_target="tpu_custom_call" | custom-call | flops 1 | bytes 1 | tf_op jit(solution)/shard_map/forward/pallas_call | solution.py:24
  32.6 8.5 forward.3.refs_0_
  45.9 20.3 %collective-permute-done = f32[4,64]{1,0:T(4,128)S(1)} collective-permute-done((f32[4,64]{1,0:T(4,128)S(1)}, f32[4,64]{1,0:T(4,128)S(1)}, u32[]{:S(2)}, u32[]{:S(2)}) %collective-permute-start) | collective-permute-done | bytes 1056 | tf_op jit(solution)/shard_map/ppermute | solution.py:542
  86.5 12.7 %collective-permute-done.6.refs_0_.refs_2_ = f32[8,128]{1,0:T(8,128)S(1)} collective-permute-done((f32[8,128]{1,0:T(8,128)S(1)}, f32[8,128]{1,0:T(8,128)S(1)}, u32[]{:S(2)}, u32[]{:S(2)}) %collective-permute-start.6) | collective-permute-done | bytes 4128 | tf_op jit(solution)/shard_map/ppermute | solution.py:451
  114.4 21.3 %collective-permute-done.14.refs_0_ = bf16[1,512,1024]{2,1,0:T(8,128)(2,1)S(1)} collective-permute-done((bf16[1,512,1024]{2,1,0:T(8,128)(2,1)}, bf16[1,512,1024]{2,1,0:T(8,128)(2,1)S(1)}, u32[]{:S(2)}, u32[]{:S(2)}) %collective-permute-start.14) | collective-permute-done | bytes 1048608 | tf_op jit(solution)/shard_map/ppermute | solution.py:450
  171.9 13.5 %collective-permute-done.16.refs_0_ = bf16[2,256,1536]{2,1,0:T(8,128)(2,1)S(1)} collective-permute-done((bf16[2,256,1536]{2,1,0:T(8,128)(2,1)}, bf16[2,256,1536]{2,1,0:T(8,128)(2,1)S(1)}, u32[]{:S(2)}, u32[]{:S(2)}) %collective-permute-start.16) | collective-permute-done | bytes 1572896 | tf_op jit(solution)/shard_map/ppermute | solution.py:450
  195.5 9.2 %cut.10 = (bf16[2,384,1536]{2,1,0:T(8,128)(2,1)}, bf16[2,384,1536]{2,1,0:T(8,128)(2,1)}) custom-call(s32[5]{0:T(128)S(1)} %stack.153.ids_ref, bf16[3584,2048]{1,0:T(8,128)(2,1)} %bitcast.72, bf16[3584,512]{1,0:T(8,128)(2,1)} %bitcast.61, bf16[2,256,1536]{2,1,0:T(8,128)(2,1)S(1)} %copy-done.10), custom_call_target="tpu_custom_call" | custom-call | flops 1 | bytes 1 | tf_op jit(solution)/shard_map/cut/pallas_call | solution.py:24
  210.8 17.1 %collective-permute-done.20.refs_1_.refs_4_.refs_5_.refs_6_.refs_7_.refs_12_.refs_13_.refs_14_.refs_15_ = bf16[4,128,1536]{2,1,0:T(8,128)(2,1)} collective-permute-done((bf16[4,128,1536]{2,1,0:T(8,128)(2,1)}, bf16[4,128,1536]{2,1,0:T(8,128)(2,1)}, u32[]{:S(2)}, u32[]{:S(2)}) %collective-permute-start.20) | collective-permute-done | bytes 1572896 | tf_op jit(solution)/shard_map/ppermute | solution.py:451
  248.0 18.2 %collective-permute-done.21.refs_1_.refs_4_.refs_5_.refs_6_.refs_7_.refs_12_.refs_13_.refs_14_.refs_15_ = bf16[4,128,1536]{2,1,0:T(8,128)(2,1)} collective-permute-done((bf16[4,128,1536]{2,1,0:T(8,128)(2,1)}, bf16[4,128,1536]{2,1,0:T(8,128)(2,1)}, u32[]{:S(2)}, u32[]{:S(2)}) %collective-permute-start.21) | collective-permute-done | bytes 1572896 | tf_op jit(solution)/shard_map/ppermute | solution.py:451
  298.7 25.8 %collective-permute-done.24.refs_1_.refs_4_.refs_5_.refs_6_.refs_7_.refs_12_.refs_13_.refs_14_.refs_15_ = bf16[4,128,1536]{2,1,0:T(8,128)(2,1)} collective-permute-done((bf16[4,128,1536]{2,1,0:T(8,128)(2,1)}, bf16[4,128,1536]{2,1,0:T(8,128)(2,1)}, u32[]{:S(2)}, u32[]{:S(2)}) %collective-permute-start.24) | collective-permute-done | bytes 1572896 | tf_op jit(solution)/shard_map/ppermute | solution.py:451
  351.7 10.7 %collective-permute-done.25.refs_1_.refs_4_.refs_5_.refs_6_.refs_7_.refs_12_.refs_13_.refs_14_.refs_15_ = bf16[4,128,1536]{2,1,0:T(8,128)(2,1)} collective-permute-done((bf16[4,128,1536]{2,1,0:T(8,128)(2,1)}, bf16[4,128,1536]{2,1,0:T(8,128)(2,1)}, u32[]{:S(2)}, u32[]{:S(2)}) %collective-permute-start.25) | collective-permute-done | bytes 1572896 | tf_op jit(solution)/shard_map/ppermute | solution.py:451
  392.1 8.3 cut.12
  405.2 13.3 %collective-permute-start.31 = (bf16[4,128,1536]{2,1,0:T(8,128)(2,1)}, bf16[4,128,1536]{2,1,0:T(8,128)(2,1)S(1)}, u32[]{:S(2)}, u32[]{:S(2)}) collective-permute-start(bf16[4,128,1536]{2,1,0:T(8,128)(2,1)} %gate.40.refs_27_), channel_id=1, source_target_pairs={{0,8},{2,10},{4,12},{6,14},{24,16},{26,18},{28,20},{30,22},{1,9},{... | collective-permute-start | bytes 4718600 | tf_op jit(solution)/shard_map/ppermute | solution.py:451
  471.9 21.8 %collective-permute-done.41.refs_5_.refs_4_.refs_6_.refs_7_ = bf16[4,128,1024]{2,1,0:T(8,128)(2,1)S(1)} collective-permute-done((bf16[4,128,1024]{2,1,0:T(8,128)(2,1)}, bf16[4,128,1024]{2,1,0:T(8,128)(2,1)S(1)}, u32[]{:S(2)}, u32[]{:S(2)}) %collective-permute-start.41) | collective-permute-done | bytes 1048608 | tf_op jit(solution)/shard_map/ppermute | solution.py:452
  536.6 8.8 collective-permute-done.36.refs_0_
  557.4 20.1 %collective-permute-done.45.refs_2_.refs_4_.refs_5_.refs_6_.refs_7_ = bf16[4,128,1024]{2,1,0:T(8,128)(2,1)} collective-permute-done((bf16[4,128,1024]{2,1,0:T(8,128)(2,1)}, bf16[4,128,1024]{2,1,0:T(8,128)(2,1)}, u32[]{:S(2)}, u32[]{:S(2)}) %collective-permute-start.45) | collective-permute-done | bytes 1048608 | tf_op jit(solution)/shard_map/ppermute | solution.py:452
  662.7 10.4 %collective-permute-start.60 = (bf16[4,128,1024]{2,1,0:T(8,128)(2,1)}, bf16[4,128,1024]{2,1,0:T(8,128)(2,1)}, u32[]{:S(2)}, u32[]{:S(2)}) collective-permute-start(bf16[4,128,1024]{2,1,0:T(8,128)(2,1)} %pack.21.refs_1_.refs_25_), channel_id=1, source_target_pairs={{0,8},{2,10},{4,12},{6,14},{8,0},{10,2},{12,4},{14,6},{16,24},{18,... | collective-permute-start | bytes 3145736 | tf_op jit(solution)/shard_map/ppermute | solution.py:452
  714.4 25.6 %collective-permute-start.65 = (bf16[4,128,1024]{2,1,0:T(8,128)(2,1)}, bf16[4,128,1024]{2,1,0:T(8,128)(2,1)}, u32[]{:S(2)}, u32[]{:S(2)}) collective-permute-start(bf16[4,128,1024]{2,1,0:T(8,128)(2,1)} %pack.22.refs_5_), channel_id=1, source_target_pairs={{0,8},{2,10},{4,12},{6,14},{8,0},{10,2},{12,4},{14,6},{16,24},{18,... | collective-permute-start | bytes 3145736 | tf_op jit(solution)/shard_map/ppermute | solution.py:452
  748.4 16.1 %collective-permute-done.65.refs_2_ = bf16[4,128,1024]{2,1,0:T(8,128)(2,1)} collective-permute-done((bf16[4,128,1024]{2,1,0:T(8,128)(2,1)}, bf16[4,128,1024]{2,1,0:T(8,128)(2,1)}, u32[]{:S(2)}, u32[]{:S(2)}) %collective-permute-start.65) | collective-permute-done | bytes 1048608 | tf_op jit(solution)/shard_map/ppermute | solution.py:452
  764.4 14.8 %collective-permute-done.66.refs_5_ = bf16[4,128,1024]{2,1,0:T(8,128)(2,1)} collective-permute-done((bf16[4,128,1024]{2,1,0:T(8,128)(2,1)}, bf16[4,128,1024]{2,1,0:T(8,128)(2,1)}, u32[]{:S(2)}, u32[]{:S(2)}) %collective-permute-start.66) | collective-permute-done | bytes 1048608 | tf_op jit(solution)/shard_map/ppermute | solution.py:452
  802.3 14.9 %collective-permute-start.73 = (bf16[4,128,1024]{2,1,0:T(8,128)(2,1)}, bf16[4,128,1024]{2,1,0:T(8,128)(2,1)}, u32[]{:S(2)}, u32[]{:S(2)}) collective-permute-start(bf16[4,128,1024]{2,1,0:T(8,128)(2,1)} %pack.26.refs_0_), channel_id=1, source_target_pairs={{0,8},{2,10},{4,12},{6,14},{8,0},{10,2},{12,4},{14,6},{16,24},{18,... | collective-permute-start | bytes 3145736 | tf_op jit(solution)/shard_map/ppermute | solution.py:452
  819.3 13.5 %collective-permute-done.71.refs_5_ = bf16[4,128,1024]{2,1,0:T(8,128)(2,1)} collective-permute-done((bf16[4,128,1024]{2,1,0:T(8,128)(2,1)S(1)}, bf16[4,128,1024]{2,1,0:T(8,128)(2,1)}, u32[]{:S(2)}, u32[]{:S(2)}) %collective-permute-start.71) | collective-permute-done | bytes 1048608 | tf_op jit(solution)/shard_map/ppermute | solution.py:452
  862.2 18.4 %collective-permute-done.69.refs_2_ = bf16[4,128,1024]{2,1,0:T(8,128)(2,1)S(1)} collective-permute-done((bf16[4,128,1024]{2,1,0:T(8,128)(2,1)S(1)}, bf16[4,128,1024]{2,1,0:T(8,128)(2,1)S(1)}, u32[]{:S(2)}, u32[]{:S(2)}) %collective-permute-start.69) | collective-permute-done | bytes 1048608 | tf_op jit(solution)/shard_map/ppermute | solution.py:452
  889.1 9.7 %collective-permute-done.77.refs_0_ = bf16[2,1,128,1024]{3,2,1,0:T(8,128)(2,1)S(1)} collective-permute-done((bf16[2,1,128,1024]{3,2,1,0:T(8,128)(2,1)S(1)}, bf16[2,1,128,1024]{3,2,1,0:T(8,128)(2,1)S(1)}, u32[]{:S(2)}, u32[]{:S(2)}) %collective-permute-start.77) | collective-permute-done | bytes 524320 | tf_op jit(solution)/shard_map/ppermute | solution.py:450
  (657 shorter events, 539.7 us)
Async XLA Ops:
  11.7 57.2 %collective-permute-start.3 = (f32[512,1024]{1,0:T(8,128)}, f32[512,1024]{1,0:T(8,128)}, u32[]{:S(2)}, u32[]{:S(2)}) collective-permute-start(f32[512,1024]{1,0:T(8,128)} %get-tuple-element.55.refs_1_), channel_id=1, source_target_pairs={{0,1},{1,0},{2,3},{3,2},{4,5},{5,4},{6,7},{7,6},{8,9},{9,8},{10,11... | collective-permute-start | bytes 6291464 | tf_op jit(solution)/shard_map/ppermute | solution.py:547
  204.7 69.2 %collective-permute-start.18 = (bf16[2,384,1536]{2,1,0:T(8,128)(2,1)}, bf16[2,384,1536]{2,1,0:T(8,128)(2,1)S(1)}, u32[]{:S(2)}, u32[]{:S(2)}) collective-permute-start(bf16[2,384,1536]{2,1,0:T(8,128)(2,1)} %get-tuple-element.64.refs_24_), channel_id=1, source_target_pairs={{0,4},{2,6},{4,0},{6,2},{8,12},{10,14},{12,8},{14,10},{16,20},{18,... | collective-permute-start | bytes 7077896 | tf_op jit(solution)/shard_map/ppermute | solution.py:450
  283.2 96.7 %collective-permute-start.29 = (bf16[4,512,1024]{2,1,0:T(8,128)(2,1)}, bf16[4,512,1024]{2,1,0:T(8,128)(2,1)}, u32[]{:S(2)}, u32[]{:S(2)}) collective-permute-start(bf16[4,512,1024]{2,1,0:T(8,128)(2,1)} %gate.38), channel_id=1, source_target_pairs={{0,1},{1,0},{2,3},{3,2},{4,5},{5,4},{6,7},{7,6},{8,9},{9,8},{10,11... | collective-permute-start | bytes 12582920 | tf_op jit(solution)/shard_map/ppermute | solution.py:577
  331.8 51.1 %collective-permute-start.28 = (bf16[12,128,512]{2,1,0:T(8,128)(2,1)}, bf16[12,128,512]{2,1,0:T(8,128)(2,1)}, u32[]{:S(2)}, u32[]{:S(2)}) collective-permute-start(bf16[12,128,512]{2,1,0:T(8,128)(2,1)} %copy-done.35), channel_id=1, source_target_pairs={{8,16},{10,18},{12,20},{14,22},{16,8},{18,10},{20,12},{22,14},{9,1... | collective-permute-start | bytes 4718600 | tf_op jit(solution)/shard_map/ppermute | solution.py:455
  379.9 139.8 %collective-permute-start.38 = (bf16[4,512,1024]{2,1,0:T(8,128)(2,1)}, bf16[4,512,1024]{2,1,0:T(8,128)(2,1)}, u32[]{:S(2)}, u32[]{:S(2)}) collective-permute-start(bf16[4,512,1024]{2,1,0:T(8,128)(2,1)} %gate.41.refs_25_), channel_id=1, source_target_pairs={{0,1},{1,0},{2,3},{3,2},{4,5},{5,4},{6,7},{7,6},{8,9},{9,8},{10,11... | collective-permute-start | bytes 12582920 | tf_op jit(solution)/shard_map/ppermute | solution.py:579
  380.6 41.9 %collective-permute-start.33 = (bf16[12,128,512]{2,1,0:T(8,128)(2,1)}, bf16[12,128,512]{2,1,0:T(8,128)(2,1)}, u32[]{:S(2)}, u32[]{:S(2)}) collective-permute-start(bf16[12,128,512]{2,1,0:T(8,128)(2,1)} %copy-done.28), channel_id=1, source_target_pairs={{8,16},{10,18},{12,20},{14,22},{16,8},{18,10},{20,12},{22,14},{9,1... | collective-permute-start | bytes 4718600 | tf_op jit(solution)/shard_map/ppermute | solution.py:455
  401.9 48.1 %collective-permute-start.32 = (bf16[12,128,512]{2,1,0:T(8,128)(2,1)}, bf16[12,128,512]{2,1,0:T(8,128)(2,1)}, u32[]{:S(2)}, u32[]{:S(2)}) collective-permute-start(bf16[12,128,512]{2,1,0:T(8,128)(2,1)} %merge_partial.18.refs_2_.refs_4_.refs_0_.mine_ref), channel_id=1, source_target_pairs={{8,16},{10,18},{12,20},{14,22},{16,8},{18,10},{20,12},{22,14},{9,1... | collective-permute-start | bytes 4718600 | tf_op jit(solution)/shard_map/ppermute | solution.py:455
  405.2 50.9 %collective-permute-start.31 = (bf16[4,128,1536]{2,1,0:T(8,128)(2,1)}, bf16[4,128,1536]{2,1,0:T(8,128)(2,1)S(1)}, u32[]{:S(2)}, u32[]{:S(2)}) collective-permute-start(bf16[4,128,1536]{2,1,0:T(8,128)(2,1)} %gate.40.refs_27_), channel_id=1, source_target_pairs={{0,8},{2,10},{4,12},{6,14},{24,16},{26,18},{28,20},{30,22},{1,9},{... | collective-permute-start | bytes 4718600 | tf_op jit(solution)/shard_map/ppermute | solution.py:451
  441.1 68.5 %collective-permute-start.40 = (bf16[2,384,1024]{2,1,0:T(8,128)(2,1)}, bf16[2,384,1024]{2,1,0:T(8,128)(2,1)}, u32[]{:S(2)}, u32[]{:S(2)}) collective-permute-start(bf16[2,384,1024]{2,1,0:T(8,128)(2,1)} %pad_maximum_fusion.10), channel_id=1, source_target_pairs={{0,2},{2,0},{4,6},{6,4},{8,10},{10,8},{12,14},{14,12},{16,18},{18,... | collective-permute-start | bytes 4718600 | tf_op jit(solution)/shard_map/ppermute | solution.py:450
  450.0 43.7 %collective-permute-start.41 = (bf16[4,128,1024]{2,1,0:T(8,128)(2,1)}, bf16[4,128,1024]{2,1,0:T(8,128)(2,1)S(1)}, u32[]{:S(2)}, u32[]{:S(2)}) collective-permute-start(bf16[4,128,1024]{2,1,0:T(8,128)(2,1)} %pack.15.refs_25_), channel_id=1, source_target_pairs={{0,8},{2,10},{4,12},{6,14},{8,0},{10,2},{12,4},{14,6},{16,24},{18,... | collective-permute-start | bytes 3145736 | tf_op jit(solution)/shard_map/ppermute | solution.py:452
  456.1 58.9 %collective-permute-start.39 = (bf16[12,128,512]{2,1,0:T(8,128)(2,1)}, bf16[12,128,512]{2,1,0:T(8,128)(2,1)}, u32[]{:S(2)}, u32[]{:S(2)}) collective-permute-start(bf16[12,128,512]{2,1,0:T(8,128)(2,1)} %merge_partial.19.refs_4_.refs_1_.mine_ref.refs_3_), channel_id=1, source_target_pairs={{8,16},{10,18},{12,20},{14,22},{16,8},{18,10},{20,12},{22,14},{9,1... | collective-permute-start | bytes 4718600 | tf_op jit(solution)/shard_map/ppermute | solution.py:455
  499.2 48.4 %collective-permute-start.43 = (bf16[12,128,512]{2,1,0:T(8,128)(2,1)}, bf16[12,128,512]{2,1,0:T(8,128)(2,1)}, u32[]{:S(2)}, u32[]{:S(2)}) collective-permute-start(bf16[12,128,512]{2,1,0:T(8,128)(2,1)} %copy-done.38), channel_id=1, source_target_pairs={{8,16},{10,18},{12,20},{14,22},{16,8},{18,10},{20,12},{22,14},{9,1... | collective-permute-start | bytes 4718600 | tf_op jit(solution)/shard_map/ppermute | solution.py:455
  532.5 45.0 %collective-permute-start.45 = (bf16[4,128,1024]{2,1,0:T(8,128)(2,1)}, bf16[4,128,1024]{2,1,0:T(8,128)(2,1)}, u32[]{:S(2)}, u32[]{:S(2)}) collective-permute-start(bf16[4,128,1024]{2,1,0:T(8,128)(2,1)} %pack.16.refs_25_), channel_id=1, source_target_pairs={{0,8},{2,10},{4,12},{6,14},{8,0},{10,2},{12,4},{14,6},{16,24},{18,... | collective-permute-start | bytes 3145736 | tf_op jit(solution)/shard_map/ppermute | solution.py:452
  532.6 66.3 %collective-permute-start.48 = (bf16[12,128,512]{2,1,0:T(8,128)(2,1)}, bf16[12,128,512]{2,1,0:T(8,128)(2,1)}, u32[]{:S(2)}, u32[]{:S(2)}) collective-permute-start(bf16[12,128,512]{2,1,0:T(8,128)(2,1)} %merge_partial.21.refs_1_.refs_4_.mine_ref.refs_3_), channel_id=1, source_target_pairs={{8,16},{10,18},{12,20},{14,22},{16,8},{18,10},{20,12},{22,14},{9,1... | collective-permute-start | bytes 4718600 | tf_op jit(solution)/shard_map/ppermute | solution.py:455
  545.4 45.4 %collective-permute-start.50 = (bf16[2,2,128,1024]{3,2,1,0:T(8,128)(2,1)}, bf16[2,2,128,1024]{3,2,1,0:T(8,128)(2,1)}, u32[]{:S(2)}, u32[]{:S(2)}) collective-permute-start(bf16[2,2,128,1024]{3,2,1,0:T(8,128)(2,1)} %pad_maximum_fusion.13), channel_id=1, source_target_pairs={{0,2},{2,0},{4,6},{6,4},{8,10},{10,8},{12,14},{14,12},{16,18},{18,... | collective-permute-start | bytes 3145736 | tf_op jit(solution)/shard_map/ppermute | solution.py:450
  547.6 62.2 %collective-permute-start.42 = (bf16[2,256,1024]{2,1,0:T(8,128)(2,1)}, bf16[2,256,1024]{2,1,0:T(8,128)(2,1)S(1)}, u32[]{:S(2)}, u32[]{:S(2)}) collective-permute-start(bf16[2,256,1024]{2,1,0:T(8,128)(2,1)} %pad_maximum_fusion.12), channel_id=1, source_target_pairs={{0,2},{2,0},{4,6},{6,4},{8,10},{10,8},{12,14},{14,12},{16,18},{18,... | collective-permute-start | bytes 3145736 | tf_op jit(solution)/shard_map/ppermute | solution.py:450
  607.9 43.0 %collective-permute-start.53 = (bf16[12,128,512]{2,1,0:T(8,128)(2,1)}, bf16[12,128,512]{2,1,0:T(8,128)(2,1)}, u32[]{:S(2)}, u32[]{:S(2)}) collective-permute-start(bf16[12,128,512]{2,1,0:T(8,128)(2,1)} %merge_partial.23.refs_4_.mine_ref.refs_3_), channel_id=1, source_target_pairs={{8,16},{10,18},{12,20},{14,22},{16,8},{18,10},{20,12},{22,14},{9,1... | collective-permute-start | bytes 4718600 | tf_op jit(solution)/shard_map/ppermute | solution.py:455
  629.1 47.2 %collective-permute-start.59 = (bf16[12,128,512]{2,1,0:T(8,128)(2,1)}, bf16[12,128,512]{2,1,0:T(8,128)(2,1)}, u32[]{:S(2)}, u32[]{:S(2)}) collective-permute-start(bf16[12,128,512]{2,1,0:T(8,128)(2,1)} %merge_partial.24.refs_6_.mine_ref.refs_0_), channel_id=1, source_target_pairs={{8,16},{10,18},{12,20},{14,22},{16,8},{18,10},{20,12},{22,14},{9,1... | collective-permute-start | bytes 4718600 | tf_op jit(solution)/shard_map/ppermute | solution.py:455
  693.0 49.9 %collective-permute-start.62 = (bf16[2,2,128,1024]{3,2,1,0:T(8,128)(2,1)S(1)}, bf16[2,2,128,1024]{3,2,1,0:T(8,128)(2,1)}, u32[]{:S(2)}, u32[]{:S(2)}) collective-permute-start(bf16[2,2,128,1024]{3,2,1,0:T(8,128)(2,1)S(1)} %get-tuple-element.84), channel_id=1, source_target_pairs={{0,4},{2,6},{4,0},{6,2},{8,12},{10,14},{12,8},{14,10},{16,20},{18,... | collective-permute-start | bytes 3145736 | tf_op jit(solution)/shard_map/ppermute | solution.py:450
  693.6 50.7 %collective-permute-start.64 = (bf16[12,128,512]{2,1,0:T(8,128)(2,1)}, bf16[12,128,512]{2,1,0:T(8,128)(2,1)}, u32[]{:S(2)}, u32[]{:S(2)}) collective-permute-start(bf16[12,128,512]{2,1,0:T(8,128)(2,1)} %copy-done.63), channel_id=1, source_target_pairs={{8,16},{10,18},{12,20},{14,22},{16,8},{18,10},{20,12},{22,14},{9,1... | collective-permute-start | bytes 4718600 | tf_op jit(solution)/shard_map/ppermute | solution.py:455
  712.6 79.6 %collective-permute-start.61 = (bf16[12,128,512]{2,1,0:T(8,128)(2,1)}, bf16[12,128,512]{2,1,0:T(8,128)(2,1)}, u32[]{:S(2)}, u32[]{:S(2)}) collective-permute-start(bf16[12,128,512]{2,1,0:T(8,128)(2,1)} %merge_partial.27.refs_0_.mine_ref.refs_3_), channel_id=1, source_target_pairs={{8,16},{10,18},{12,20},{14,22},{16,8},{18,10},{20,12},{22,14},{9,1... | collective-permute-start | bytes 4718600 | tf_op jit(solution)/shard_map/ppermute | solution.py:455
  714.4 50.0 %collective-permute-start.65 = (bf16[4,128,1024]{2,1,0:T(8,128)(2,1)}, bf16[4,128,1024]{2,1,0:T(8,128)(2,1)}, u32[]{:S(2)}, u32[]{:S(2)}) collective-permute-start(bf16[4,128,1024]{2,1,0:T(8,128)(2,1)} %pack.22.refs_5_), channel_id=1, source_target_pairs={{0,8},{2,10},{4,12},{6,14},{8,0},{10,2},{12,4},{14,6},{16,24},{18,... | collective-permute-start | bytes 3145736 | tf_op jit(solution)/shard_map/ppermute | solution.py:452
  744.2 42.9 %collective-permute-start.63 = (bf16[2,2,128,1024]{3,2,1,0:T(8,128)(2,1)S(1)}, bf16[2,2,128,1024]{3,2,1,0:T(8,128)(2,1)S(1)}, u32[]{:S(2)}, u32[]{:S(2)}) collective-permute-start(bf16[2,2,128,1024]{3,2,1,0:T(8,128)(2,1)S(1)} %pad_maximum_fusion.16), channel_id=1, source_target_pairs={{0,2},{2,0},{4,6},{6,4},{8,10},{10,8},{12,14},{14,12},{16,18},{18,... | collective-permute-start | bytes 3145736 | tf_op jit(solution)/shard_map/ppermute | solution.py:450
  802.3 45.4 %collective-permute-start.73 = (bf16[4,128,1024]{2,1,0:T(8,128)(2,1)}, bf16[4,128,1024]{2,1,0:T(8,128)(2,1)}, u32[]{:S(2)}, u32[]{:S(2)}) collective-permute-start(bf16[4,128,1024]{2,1,0:T(8,128)(2,1)} %pack.26.refs_0_), channel_id=1, source_target_pairs={{0,8},{2,10},{4,12},{6,14},{8,0},{10,2},{12,4},{14,6},{16,24},{18,... | collective-permute-start | bytes 3145736 | tf_op jit(solution)/shard_map/ppermute | solution.py:452
  (215 other events, 2816.6 us)

commit v3 on v2

--- a/solution.py
+++ b/solution.py
@@ -582,7 +582,7 @@
 
     if fine:
         lift(1, [lifts[0][1]])
-        before[0].append(lifts[1][0])
+        before[0].append(lifts[1][1])
     else:
         last = early[0]
         for j in range(1, shards):
@@ -668,6 +668,8 @@
             buffer = merge(t, upper, None, planes, buffer, before[t])
         chain = sent[t] = buffer
         got[t] = hub_to_hub(buffer)
+        if fine and t < 2:
+            before[t + 1].append(got[t])
         if len(waiting) == 2:
             pick(t)
         if t >= 4:

time: 916 us -> 904 us (0.987)
  starting transfers between devices: 201 us -> 188 us
  local copies, waits for them, and re-layouts: 101 us -> 111 us
    unnamed x318 -> x342, local copies, waits for them, and re-layouts: 46.7 us -> 55.6 us
  transfers between devices with their start and end apart: 81 -> 81, of which waited for: 28 -> 31; matrix products, arithmetic and copies ran while one was open for 9% -> 9% of each run, Pallas kernels for 29% -> 29%
where the time goes in v3:
time: 904 us; the launch traced here: 891 us
  waiting for transfers between devices  291 us (32%)
  Pallas kernels  270 us (30%)
  starting transfers between devices  188 us (21%)
  local copies, waits for them, and re-layouts  111 us (12%)
  other arithmetic  29.1 us (3%)
    pallas_call x68, Pallas kernels, call(): pl.pallas_call(kernel, out_shape=out_shape, grid_spec=pltpu.PrefetchScala...  270 us
    ppermute x14, waiting for transfers between devices, body(): lax.ppermute(array, 'client', between([(0, 1), (1, 0), (2, 3), (3, 2)]))  127 us
    ppermute x9, waiting for transfers between devices, body(): lax.ppermute(array, 'client', between([(0, 1), (3, 2)]))  85 us
    ppermute x14, starting transfers between devices, body(): lax.ppermute(array, 'client', between([(0, 1), (1, 0), (2, 3), (3, 2)]))  77.3 us
    ppermute x36, waiting for transfers between devices, body(): to_peer = lambda array, k: lax.ppermute(array, 'client', swap(k))  57.5 us
    unnamed x342, local copies, waits for them, and re-layouts  55.6 us
    ppermute x9, starting transfers between devices, body(): lax.ppermute(array, 'client', between([(0, 1), (3, 2)]))  50.5 us
    ppermute x16, starting transfers between devices, body(): lax.ppermute(array, 'client', between([(1, 2), (2, 1)]))  27.8 us
  transfers between devices with their start and end apart: 81, of which 31 were waited for; matrix products, arithmetic and copies ran while one was open for 9% of the time, Pallas kernels for 29%

profile of v3, /device:TPU:0, one launch (start us, length us, event | category | flops | bytes accessed | tf_op | source)
XLA Modules:
  0.0 891.2 jit_solution(13728867868810221173)
XLA Ops:
  1.3 10.4 %forward.2 = (f32[512,1024]{1,0:T(8,128)}, f32[4,128,128]{2,1,0:T(8,128)S(1)}) custom-call(s32[2]{0:T(128)S(1)} %pad_add_fusion.2.ids_ref, bf16[512,3584]{1,0:T(8,128)(2,1)} %bitcast.74, bf16[3584,2048]{1,0:T(8,128)(2,1)} %bitcast.65, bf16[4,64,2048]{2,1,0:T(8,128)(2,1)S(1)} %bitcast.63), custom_call_target="tpu_custom_call" | custom-call | flops 1 | bytes 1 | tf_op jit(solution)/shard_map/forward/pallas_call | solution.py:24
  32.6 8.5 forward.3.refs_0_
  45.9 20.4 %collective-permute-done = f32[4,64]{1,0:T(4,128)S(1)} collective-permute-done((f32[4,64]{1,0:T(4,128)S(1)}, f32[4,64]{1,0:T(4,128)S(1)}, u32[]{:S(2)}, u32[]{:S(2)}) %collective-permute-start) | collective-permute-done | bytes 1056 | tf_op jit(solution)/shard_map/ppermute | solution.py:542
  85.4 14.5 %collective-permute-done.6.refs_0_.refs_2_ = f32[8,128]{1,0:T(8,128)S(1)} collective-permute-done((f32[8,128]{1,0:T(8,128)S(1)}, f32[8,128]{1,0:T(8,128)S(1)}, u32[]{:S(2)}, u32[]{:S(2)}) %collective-permute-start.6) | collective-permute-done | bytes 4128 | tf_op jit(solution)/shard_map/ppermute | solution.py:451
  116.0 19.5 %collective-permute-done.14.refs_0_ = bf16[1,512,1024]{2,1,0:T(8,128)(2,1)S(1)} collective-permute-done((bf16[1,512,1024]{2,1,0:T(8,128)(2,1)}, bf16[1,512,1024]{2,1,0:T(8,128)(2,1)S(1)}, u32[]{:S(2)}, u32[]{:S(2)}) %collective-permute-start.14) | collective-permute-done | bytes 1048608 | tf_op jit(solution)/shard_map/ppermute | solution.py:450
  170.1 13.5 %collective-permute-done.18.refs_24_.refs_1_.refs_4_.refs_5_.refs_6_.refs_7_.refs_12_.refs_13_.refs_14_.refs_15_ = bf16[4,128,1536]{2,1,0:T(8,128)(2,1)S(1)} collective-permute-done((bf16[4,128,1536]{2,1,0:T(8,128)(2,1)}, bf16[4,128,1536]{2,1,0:T(8,128)(2,1)S(1)}, u32[]{:S(2)}, u32[]{:S(2)}) %collective-permute-start.18) | collective-permute-done | bytes 1572896 | tf_op jit(solution)/shard_map/ppermute | solution.py:451
  199.6 9.2 %cut.10 = (bf16[2,384,1536]{2,1,0:T(8,128)(2,1)}, bf16[2,384,1536]{2,1,0:T(8,128)(2,1)}) custom-call(s32[5]{0:T(128)S(1)} %stack.153.ids_ref, bf16[3584,2048]{1,0:T(8,128)(2,1)} %bitcast.70, bf16[3584,512]{1,0:T(8,128)(2,1)} %bitcast.61, bf16[2,256,1536]{2,1,0:T(8,128)(2,1)} %gate.32.refs_1_.refs_2_.refs_10_), custom_call_target="tpu_custom_call" | custom-call | flops 1 | bytes 1 | tf_op jit(solution)/shard_map/cut/pallas_call | solution.py:24
  238.9 15.0 %collective-permute-done.21.refs_1_.refs_4_.refs_5_.refs_6_.refs_7_.refs_12_.refs_13_.refs_14_.refs_15_ = bf16[4,128,1536]{2,1,0:T(8,128)(2,1)} collective-permute-done((bf16[4,128,1536]{2,1,0:T(8,128)(2,1)}, bf16[4,128,1536]{2,1,0:T(8,128)(2,1)}, u32[]{:S(2)}, u32[]{:S(2)}) %collective-permute-start.21) | collective-permute-done | bytes 1572896 | tf_op jit(solution)/shard_map/ppermute | solution.py:451
  271.6 9.0 %collective-permute-start.25 = (bf16[4,128,1536]{2,1,0:T(8,128)(2,1)}, bf16[4,128,1536]{2,1,0:T(8,128)(2,1)S(1)}, u32[]{:S(2)}, u32[]{:S(2)}) collective-permute-start(bf16[4,128,1536]{2,1,0:T(8,128)(2,1)} %gate.34.refs_26_), channel_id=1, source_target_pairs={{0,8},{2,10},{4,12},{6,14},{24,16},{26,18},{28,20},{30,22},{1,9},{... | collective-permute-start | bytes 4718600 | tf_op jit(solution)/shard_map/ppermute | solution.py:451
  289.1 25.7 %collective-permute-done.25.refs_1_.refs_4_.refs_5_.refs_6_.refs_7_.refs_12_.refs_13_.refs_14_.refs_15_ = bf16[4,128,1536]{2,1,0:T(8,128)(2,1)S(1)} collective-permute-done((bf16[4,128,1536]{2,1,0:T(8,128)(2,1)}, bf16[4,128,1536]{2,1,0:T(8,128)(2,1)S(1)}, u32[]{:S(2)}, u32[]{:S(2)}) %collective-permute-start.25) | collective-permute-done | bytes 1572896 | tf_op jit(solution)/shard_map/ppermute | solution.py:451
  340.3 13.6 %collective-permute-done.26.refs_1_.refs_4_.refs_5_.refs_6_.refs_7_.refs_12_.refs_13_.refs_14_.refs_15_ = bf16[4,128,1536]{2,1,0:T(8,128)(2,1)S(1)} collective-permute-done((bf16[4,128,1536]{2,1,0:T(8,128)(2,1)}, bf16[4,128,1536]{2,1,0:T(8,128)(2,1)S(1)}, u32[]{:S(2)}, u32[]{:S(2)}) %collective-permute-start.26) | collective-permute-done | bytes 1572896 | tf_op jit(solution)/shard_map/ppermute | solution.py:451
  381.0 8.2 cut.12
  395.3 10.8 %collective-permute-start.31 = (bf16[4,128,1536]{2,1,0:T(8,128)(2,1)}, bf16[4,128,1536]{2,1,0:T(8,128)(2,1)}, u32[]{:S(2)}, u32[]{:S(2)}) collective-permute-start(bf16[4,128,1536]{2,1,0:T(8,128)(2,1)} %gate.40.refs_27_), channel_id=1, source_target_pairs={{0,8},{2,10},{4,12},{6,14},{24,16},{26,18},{28,20},{30,22},{1,9},{... | collective-permute-start | bytes 4718600 | tf_op jit(solution)/shard_map/ppermute | solution.py:451
  460.6 21.6 %collective-permute-done.41.refs_5_.refs_4_.refs_6_.refs_7_ = bf16[4,128,1024]{2,1,0:T(8,128)(2,1)S(1)} collective-permute-done((bf16[4,128,1024]{2,1,0:T(8,128)(2,1)S(1)}, bf16[4,128,1024]{2,1,0:T(8,128)(2,1)S(1)}, u32[]{:S(2)}, u32[]{:S(2)}) %collective-permute-start.41) | collective-permute-done | bytes 1048608 | tf_op jit(solution)/shard_map/ppermute | solution.py:452
  524.3 8.8 collective-permute-done.36.refs_0_
  545.5 18.7 %collective-permute-done.45.refs_2_.refs_4_.refs_5_.refs_6_.refs_7_ = bf16[4,128,1024]{2,1,0:T(8,128)(2,1)} collective-permute-done((bf16[4,128,1024]{2,1,0:T(8,128)(2,1)}, bf16[4,128,1024]{2,1,0:T(8,128)(2,1)}, u32[]{:S(2)}, u32[]{:S(2)}) %collective-permute-start.45) | collective-permute-done | bytes 1048608 | tf_op jit(solution)/shard_map/ppermute | solution.py:452
  649.1 8.4 collective-permute-start.60
  700.4 26.0 %collective-permute-start.65 = (bf16[4,128,1024]{2,1,0:T(8,128)(2,1)}, bf16[4,128,1024]{2,1,0:T(8,128)(2,1)}, u32[]{:S(2)}, u32[]{:S(2)}) collective-permute-start(bf16[4,128,1024]{2,1,0:T(8,128)(2,1)} %pack.22.refs_5_), channel_id=1, source_target_pairs={{0,8},{2,10},{4,12},{6,14},{8,0},{10,2},{12,4},{14,6},{16,24},{18,... | collective-permute-start | bytes 3145736 | tf_op jit(solution)/shard_map/ppermute | solution.py:452
  736.6 14.3 %collective-permute-done.65.refs_2_ = bf16[4,128,1024]{2,1,0:T(8,128)(2,1)} collective-permute-done((bf16[4,128,1024]{2,1,0:T(8,128)(2,1)}, bf16[4,128,1024]{2,1,0:T(8,128)(2,1)}, u32[]{:S(2)}, u32[]{:S(2)}) %collective-permute-start.65) | collective-permute-done | bytes 1048608 | tf_op jit(solution)/shard_map/ppermute | solution.py:452
  750.9 14.4 %collective-permute-done.66.refs_5_ = bf16[4,128,1024]{2,1,0:T(8,128)(2,1)} collective-permute-done((bf16[4,128,1024]{2,1,0:T(8,128)(2,1)S(1)}, bf16[4,128,1024]{2,1,0:T(8,128)(2,1)}, u32[]{:S(2)}, u32[]{:S(2)}) %collective-permute-start.66) | collective-permute-done | bytes 1048608 | tf_op jit(solution)/shard_map/ppermute | solution.py:452
  790.2 11.7 %collective-permute-start.73 = (bf16[4,128,1024]{2,1,0:T(8,128)(2,1)}, bf16[4,128,1024]{2,1,0:T(8,128)(2,1)}, u32[]{:S(2)}, u32[]{:S(2)}) collective-permute-start(bf16[4,128,1024]{2,1,0:T(8,128)(2,1)} %pack.26.refs_0_), channel_id=1, source_target_pairs={{0,8},{2,10},{4,12},{6,14},{8,0},{10,2},{12,4},{14,6},{16,24},{18,... | collective-permute-start | bytes 3145736 | tf_op jit(solution)/shard_map/ppermute | solution.py:452
  804.9 16.4 %collective-permute-done.71.refs_5_ = bf16[4,128,1024]{2,1,0:T(8,128)(2,1)S(1)} collective-permute-done((bf16[4,128,1024]{2,1,0:T(8,128)(2,1)S(1)}, bf16[4,128,1024]{2,1,0:T(8,128)(2,1)S(1)}, u32[]{:S(2)}, u32[]{:S(2)}) %collective-permute-start.71) | collective-permute-done | bytes 1048608 | tf_op jit(solution)/shard_map/ppermute | solution.py:452
  848.2 17.9 %collective-permute-done.69.refs_2_ = bf16[4,128,1024]{2,1,0:T(8,128)(2,1)S(1)} collective-permute-done((bf16[4,128,1024]{2,1,0:T(8,128)(2,1)S(1)}, bf16[4,128,1024]{2,1,0:T(8,128)(2,1)S(1)}, u32[]{:S(2)}, u32[]{:S(2)}) %collective-permute-start.69) | collective-permute-done | bytes 1048608 | tf_op jit(solution)/shard_map/ppermute | solution.py:452
  875.0 9.7 %collective-permute-done.77.refs_0_ = bf16[2,1,128,1024]{3,2,1,0:T(8,128)(2,1)S(1)} collective-permute-done((bf16[2,1,128,1024]{3,2,1,0:T(8,128)(2,1)S(1)}, bf16[2,1,128,1024]{3,2,1,0:T(8,128)(2,1)S(1)}, u32[]{:S(2)}, u32[]{:S(2)}) %collective-permute-start.77) | collective-permute-done | bytes 524320 | tf_op jit(solution)/shard_map/ppermute | solution.py:450
  (681 shorter events, 542.9 us)
Async XLA Ops:
  11.7 57.2 %collective-permute-start.3 = (f32[512,1024]{1,0:T(8,128)}, f32[512,1024]{1,0:T(8,128)}, u32[]{:S(2)}, u32[]{:S(2)}) collective-permute-start(f32[512,1024]{1,0:T(8,128)} %get-tuple-element.55.refs_1_), channel_id=1, source_target_pairs={{0,1},{1,0},{2,3},{3,2},{4,5},{5,4},{6,7},{7,6},{8,9},{9,8},{10,11... | collective-permute-start | bytes 6291464 | tf_op jit(solution)/shard_map/ppermute | solution.py:547
  208.8 53.5 %collective-permute-start.19 = (bf16[2,384,1536]{2,1,0:T(8,128)(2,1)}, bf16[2,384,1536]{2,1,0:T(8,128)(2,1)}, u32[]{:S(2)}, u32[]{:S(2)}) collective-permute-start(bf16[2,384,1536]{2,1,0:T(8,128)(2,1)} %get-tuple-element.64.refs_25_), channel_id=1, source_target_pairs={{0,4},{2,6},{4,0},{6,2},{8,12},{10,14},{12,8},{14,10},{16,20},{18,... | collective-permute-start | bytes 7077896 | tf_op jit(solution)/shard_map/ppermute | solution.py:450
  270.1 98.2 %collective-permute-start.29 = (bf16[4,512,1024]{2,1,0:T(8,128)(2,1)}, bf16[4,512,1024]{2,1,0:T(8,128)(2,1)}, u32[]{:S(2)}, u32[]{:S(2)}) collective-permute-start(bf16[4,512,1024]{2,1,0:T(8,128)(2,1)} %gate.38), channel_id=1, source_target_pairs={{0,1},{1,0},{2,3},{3,2},{4,5},{5,4},{6,7},{7,6},{8,9},{9,8},{10,11... | collective-permute-start | bytes 12582920 | tf_op jit(solution)/shard_map/ppermute | solution.py:577
  271.6 43.2 %collective-permute-start.25 = (bf16[4,128,1536]{2,1,0:T(8,128)(2,1)}, bf16[4,128,1536]{2,1,0:T(8,128)(2,1)S(1)}, u32[]{:S(2)}, u32[]{:S(2)}) collective-permute-start(bf16[4,128,1536]{2,1,0:T(8,128)(2,1)} %gate.34.refs_26_), channel_id=1, source_target_pairs={{0,8},{2,10},{4,12},{6,14},{24,16},{26,18},{28,20},{30,22},{1,9},{... | collective-permute-start | bytes 4718600 | tf_op jit(solution)/shard_map/ppermute | solution.py:451
  320.4 50.4 %collective-permute-start.28 = (bf16[12,128,512]{2,1,0:T(8,128)(2,1)}, bf16[12,128,512]{2,1,0:T(8,128)(2,1)}, u32[]{:S(2)}, u32[]{:S(2)}) collective-permute-start(bf16[12,128,512]{2,1,0:T(8,128)(2,1)} %copy-done.42), channel_id=1, source_target_pairs={{8,16},{10,18},{12,20},{14,22},{16,8},{18,10},{20,12},{22,14},{9,1... | collective-permute-start | bytes 4718600 | tf_op jit(solution)/shard_map/ppermute | solution.py:455
  368.3 138.4 %collective-permute-start.38 = (bf16[4,512,1024]{2,1,0:T(8,128)(2,1)}, bf16[4,512,1024]{2,1,0:T(8,128)(2,1)}, u32[]{:S(2)}, u32[]{:S(2)}) collective-permute-start(bf16[4,512,1024]{2,1,0:T(8,128)(2,1)} %gate.41.refs_25_), channel_id=1, source_target_pairs={{0,1},{1,0},{2,3},{3,2},{4,5},{5,4},{6,7},{7,6},{8,9},{9,8},{10,11... | collective-permute-start | bytes 12582920 | tf_op jit(solution)/shard_map/ppermute | solution.py:579
  368.9 42.5 %collective-permute-start.33 = (bf16[12,128,512]{2,1,0:T(8,128)(2,1)}, bf16[12,128,512]{2,1,0:T(8,128)(2,1)}, u32[]{:S(2)}, u32[]{:S(2)}) collective-permute-start(bf16[12,128,512]{2,1,0:T(8,128)(2,1)} %copy-done.32), channel_id=1, source_target_pairs={{8,16},{10,18},{12,20},{14,22},{16,8},{18,10},{20,12},{22,14},{9,1... | collective-permute-start | bytes 4718600 | tf_op jit(solution)/shard_map/ppermute | solution.py:455
  392.1 45.5 %collective-permute-start.32 = (bf16[12,128,512]{2,1,0:T(8,128)(2,1)}, bf16[12,128,512]{2,1,0:T(8,128)(2,1)}, u32[]{:S(2)}, u32[]{:S(2)}) collective-permute-start(bf16[12,128,512]{2,1,0:T(8,128)(2,1)} %merge_partial.18.refs_2_.refs_4_.refs_0_.mine_ref), channel_id=1, source_target_pairs={{8,16},{10,18},{12,20},{14,22},{16,8},{18,10},{20,12},{22,14},{9,1... | collective-permute-start | bytes 4718600 | tf_op jit(solution)/shard_map/ppermute | solution.py:455
  395.3 48.4 %collective-permute-start.31 = (bf16[4,128,1536]{2,1,0:T(8,128)(2,1)}, bf16[4,128,1536]{2,1,0:T(8,128)(2,1)}, u32[]{:S(2)}, u32[]{:S(2)}) collective-permute-start(bf16[4,128,1536]{2,1,0:T(8,128)(2,1)} %gate.40.refs_27_), channel_id=1, source_target_pairs={{0,8},{2,10},{4,12},{6,14},{24,16},{26,18},{28,20},{30,22},{1,9},{... | collective-permute-start | bytes 4718600 | tf_op jit(solution)/shard_map/ppermute | solution.py:451
  429.8 67.5 %collective-permute-start.40 = (bf16[2,384,1024]{2,1,0:T(8,128)(2,1)}, bf16[2,384,1024]{2,1,0:T(8,128)(2,1)S(1)}, u32[]{:S(2)}, u32[]{:S(2)}) collective-permute-start(bf16[2,384,1024]{2,1,0:T(8,128)(2,1)} %pad_maximum_fusion.10), channel_id=1, source_target_pairs={{0,2},{2,0},{4,6},{6,4},{8,10},{10,8},{12,14},{14,12},{16,18},{18,... | collective-permute-start | bytes 4718600 | tf_op jit(solution)/shard_map/ppermute | solution.py:450
  437.6 44.6 %collective-permute-start.41 = (bf16[4,128,1024]{2,1,0:T(8,128)(2,1)S(1)}, bf16[4,128,1024]{2,1,0:T(8,128)(2,1)S(1)}, u32[]{:S(2)}, u32[]{:S(2)}) collective-permute-start(bf16[4,128,1024]{2,1,0:T(8,128)(2,1)S(1)} %pack.15.refs_25_), channel_id=1, source_target_pairs={{0,8},{2,10},{4,12},{6,14},{8,0},{10,2},{12,4},{14,6},{16,24},{18,... | collective-permute-start | bytes 3145736 | tf_op jit(solution)/shard_map/ppermute | solution.py:452
  443.7 57.9 %collective-permute-start.39 = (bf16[12,128,512]{2,1,0:T(8,128)(2,1)}, bf16[12,128,512]{2,1,0:T(8,128)(2,1)}, u32[]{:S(2)}, u32[]{:S(2)}) collective-permute-start(bf16[12,128,512]{2,1,0:T(8,128)(2,1)} %merge_partial.19.refs_4_.refs_1_.mine_ref.refs_3_), channel_id=1, source_target_pairs={{8,16},{10,18},{12,20},{14,22},{16,8},{18,10},{20,12},{22,14},{9,1... | collective-permute-start | bytes 4718600 | tf_op jit(solution)/shard_map/ppermute | solution.py:455
  486.8 48.4 %collective-permute-start.43 = (bf16[12,128,512]{2,1,0:T(8,128)(2,1)}, bf16[12,128,512]{2,1,0:T(8,128)(2,1)}, u32[]{:S(2)}, u32[]{:S(2)}) collective-permute-start(bf16[12,128,512]{2,1,0:T(8,128)(2,1)} %copy-done.45), channel_id=1, source_target_pairs={{8,16},{10,18},{12,20},{14,22},{16,8},{18,10},{20,12},{22,14},{9,1... | collective-permute-start | bytes 4718600 | tf_op jit(solution)/shard_map/ppermute | solution.py:455
  519.9 44.3 %collective-permute-start.45 = (bf16[4,128,1024]{2,1,0:T(8,128)(2,1)}, bf16[4,128,1024]{2,1,0:T(8,128)(2,1)}, u32[]{:S(2)}, u32[]{:S(2)}) collective-permute-start(bf16[4,128,1024]{2,1,0:T(8,128)(2,1)} %pack.16.refs_25_), channel_id=1, source_target_pairs={{0,8},{2,10},{4,12},{6,14},{8,0},{10,2},{12,4},{14,6},{16,24},{18,... | collective-permute-start | bytes 3145736 | tf_op jit(solution)/shard_map/ppermute | solution.py:452
  519.9 66.6 %collective-permute-start.48 = (bf16[12,128,512]{2,1,0:T(8,128)(2,1)}, bf16[12,128,512]{2,1,0:T(8,128)(2,1)}, u32[]{:S(2)}, u32[]{:S(2)}) collective-permute-start(bf16[12,128,512]{2,1,0:T(8,128)(2,1)} %merge_partial.21.refs_1_.refs_4_.mine_ref.refs_3_), channel_id=1, source_target_pairs={{8,16},{10,18},{12,20},{14,22},{16,8},{18,10},{20,12},{22,14},{9,1... | collective-permute-start | bytes 4718600 | tf_op jit(solution)/shard_map/ppermute | solution.py:455
  533.1 44.5 %collective-permute-start.50 = (bf16[2,2,128,1024]{3,2,1,0:T(8,128)(2,1)}, bf16[2,2,128,1024]{3,2,1,0:T(8,128)(2,1)}, u32[]{:S(2)}, u32[]{:S(2)}) collective-permute-start(bf16[2,2,128,1024]{3,2,1,0:T(8,128)(2,1)} %pad_maximum_fusion.13), channel_id=1, source_target_pairs={{0,2},{2,0},{4,6},{6,4},{8,10},{10,8},{12,14},{14,12},{16,18},{18,... | collective-permute-start | bytes 3145736 | tf_op jit(solution)/shard_map/ppermute | solution.py:450
  535.2 62.5 %collective-permute-start.42 = (bf16[2,256,1024]{2,1,0:T(8,128)(2,1)}, bf16[2,256,1024]{2,1,0:T(8,128)(2,1)}, u32[]{:S(2)}, u32[]{:S(2)}) collective-permute-start(bf16[2,256,1024]{2,1,0:T(8,128)(2,1)} %pad_maximum_fusion.12), channel_id=1, source_target_pairs={{0,2},{2,0},{4,6},{6,4},{8,10},{10,8},{12,14},{14,12},{16,18},{18,... | collective-permute-start | bytes 3145736 | tf_op jit(solution)/shard_map/ppermute | solution.py:450
  595.8 42.6 %collective-permute-start.53 = (bf16[12,128,512]{2,1,0:T(8,128)(2,1)}, bf16[12,128,512]{2,1,0:T(8,128)(2,1)}, u32[]{:S(2)}, u32[]{:S(2)}) collective-permute-start(bf16[12,128,512]{2,1,0:T(8,128)(2,1)} %merge_partial.23.refs_4_.mine_ref.refs_3_), channel_id=1, source_target_pairs={{8,16},{10,18},{12,20},{14,22},{16,8},{18,10},{20,12},{22,14},{9,1... | collective-permute-start | bytes 4718600 | tf_op jit(solution)/shard_map/ppermute | solution.py:455
  614.3 47.5 %collective-permute-start.59 = (bf16[12,128,512]{2,1,0:T(8,128)(2,1)}, bf16[12,128,512]{2,1,0:T(8,128)(2,1)}, u32[]{:S(2)}, u32[]{:S(2)}) collective-permute-start(bf16[12,128,512]{2,1,0:T(8,128)(2,1)} %merge_partial.24.refs_6_.mine_ref.refs_0_), channel_id=1, source_target_pairs={{8,16},{10,18},{12,20},{14,22},{16,8},{18,10},{20,12},{22,14},{9,1... | collective-permute-start | bytes 4718600 | tf_op jit(solution)/shard_map/ppermute | solution.py:455
  678.9 50.3 %collective-permute-start.62 = (bf16[2,2,128,1024]{3,2,1,0:T(8,128)(2,1)}, bf16[2,2,128,1024]{3,2,1,0:T(8,128)(2,1)}, u32[]{:S(2)}, u32[]{:S(2)}) collective-permute-start(bf16[2,2,128,1024]{3,2,1,0:T(8,128)(2,1)} %get-tuple-element.84), channel_id=1, source_target_pairs={{0,4},{2,6},{4,0},{6,2},{8,12},{10,14},{12,8},{14,10},{16,20},{18,... | collective-permute-start | bytes 3145736 | tf_op jit(solution)/shard_map/ppermute | solution.py:450
  680.0 52.4 %collective-permute-start.64 = (bf16[12,128,512]{2,1,0:T(8,128)(2,1)}, bf16[12,128,512]{2,1,0:T(8,128)(2,1)}, u32[]{:S(2)}, u32[]{:S(2)}) collective-permute-start(bf16[12,128,512]{2,1,0:T(8,128)(2,1)} %copy-done.69), channel_id=1, source_target_pairs={{8,16},{10,18},{12,20},{14,22},{16,8},{18,10},{20,12},{22,14},{9,1... | collective-permute-start | bytes 4718600 | tf_op jit(solution)/shard_map/ppermute | solution.py:455
  698.6 80.8 %collective-permute-start.61 = (bf16[12,128,512]{2,1,0:T(8,128)(2,1)}, bf16[12,128,512]{2,1,0:T(8,128)(2,1)}, u32[]{:S(2)}, u32[]{:S(2)}) collective-permute-start(bf16[12,128,512]{2,1,0:T(8,128)(2,1)} %merge_partial.27.refs_0_.mine_ref.refs_3_), channel_id=1, source_target_pairs={{8,16},{10,18},{12,20},{14,22},{16,8},{18,10},{20,12},{22,14},{9,1... | collective-permute-start | bytes 4718600 | tf_op jit(solution)/shard_map/ppermute | solution.py:455
  700.4 50.4 %collective-permute-start.65 = (bf16[4,128,1024]{2,1,0:T(8,128)(2,1)}, bf16[4,128,1024]{2,1,0:T(8,128)(2,1)}, u32[]{:S(2)}, u32[]{:S(2)}) collective-permute-start(bf16[4,128,1024]{2,1,0:T(8,128)(2,1)} %pack.22.refs_5_), channel_id=1, source_target_pairs={{0,8},{2,10},{4,12},{6,14},{8,0},{10,2},{12,4},{14,6},{16,24},{18,... | collective-permute-start | bytes 3145736 | tf_op jit(solution)/shard_map/ppermute | solution.py:452
  790.2 44.6 %collective-permute-start.73 = (bf16[4,128,1024]{2,1,0:T(8,128)(2,1)}, bf16[4,128,1024]{2,1,0:T(8,128)(2,1)}, u32[]{:S(2)}, u32[]{:S(2)}) collective-permute-start(bf16[4,128,1024]{2,1,0:T(8,128)(2,1)} %pack.26.refs_0_), channel_id=1, source_target_pairs={{0,8},{2,10},{4,12},{6,14},{8,0},{10,2},{12,4},{14,6},{16,24},{18,... | collective-permute-start | bytes 3145736 | tf_op jit(solution)/shard_map/ppermute | solution.py:452
  (227 other events, 2991.1 us)
